TPU v7x, 128 devices: a whole 4x4x4 slice. The times are simulated.
128 devices in a mesh: lat: 16 (over y, z_lo, core), mp: 8 (over x, z_hi).
Axes of the slice: x: 4, y: 4, z: 4 (z_hi: 2, z_lo: 2; z = z_hi * 2 + z_lo), core: 2. Of those that a mesh axis runs over, the one named last changes fastest.
Arguments:
- fields: bfloat16 [192, 288, 512], P('lat', None, 'mp'), may hold values from -16 to 16
- first_gain: float32 [512], P('mp'), may hold values from 0.1 to 1.9
- qkv_weight: bfloat16 [512, 3, 512], P(None, None, 'mp'), may hold values from -1 to 1
- proj_weight: bfloat16 [512, 512], P(None, 'mp'), may hold values from -0.25 to 0.25
- merge_gain: float32 [4, 512], P(None, 'mp'), may hold values from 0.1 to 1.9
- merge_weight: bfloat16 [4, 512, 1024], P(None, 'mp'), may hold values from -0.125 to 0.125
- mlp_gain: float32 [1024], replicated, may hold values from 0.1 to 1.9
- up_weight: bfloat16 [1024, 4096], P(None, 'mp'), may hold values from -0.1875 to 0.1875
- down_weight: bfloat16 [1024, 4096], P(None, 'mp'), may hold values from -0.09375 to 0.09375
- expand_weight: bfloat16 [1024, 4, 512], P(None, None, 'mp'), may hold values from -0.1875 to 0.1875
- lat_shift: int32 [1], replicated, may hold values from 1 to 5
- lon_shift: int32 [1], replicated, may hold values from 1 to 11
- cotangent: bfloat16 [192, 288, 512], P('lat', None, 'mp'), may hold values from -6 to 6
Outputs:
- decoded: bfloat16 [192, 288, 512], P('lat', None, 'mp')
- grad_input: float32 [192, 288, 512], P('lat', None, 'mp')
- grad_qkv: float32 [512, 3, 512], P('lat', None, 'mp')
- grad_proj: float32 [512, 512], P('lat', 'mp')
- grad_up: float32 [1024, 4096], P('lat', 'mp')
- grad_down: float32 [1024, 4096], P('lat', 'mp')
All inputs are finite; a program needn't handle non-finite values.
Results may differ from a plain program's by a relative error of at most 0.035.
Values may be sent and summed in bfloat16 or wider, within the bound.
A program may use at most 128 MiB of HBM per device.

v0:
```python
import jax
import jax.numpy as jnp
from jax import lax
from jax.sharding import PartitionSpec as P

WIN_H = 6
WIN_W = 12
HDIM = 64


EPSILON = 1e-05
MASKED = -1e30


def passed_along(value, axis, steps):
    count = lax.axis_size(axis)
    pairs = [(source, (source + steps) % count) for source in range(count)]
    return lax.ppermute(value, axis, pairs)


def to_windows(grid):
    row_count, lon_count = (grid.shape[0], grid.shape[1])
    trailing = grid.shape[2:]
    view = grid.reshape((row_count // WIN_H, WIN_H, lon_count // WIN_W, WIN_W) + trailing)
    view = jnp.swapaxes(view, 1, 2)
    return view.reshape((row_count // WIN_H, lon_count // WIN_W, WIN_H * WIN_W) + trailing)


def from_windows(windows):
    bands, columns = (windows.shape[0], windows.shape[1])
    trailing = windows.shape[3:]
    view = windows.reshape((bands, columns, WIN_H, WIN_W) + trailing)
    view = jnp.swapaxes(view, 1, 2)
    return view.reshape((bands * WIN_H, columns * WIN_W) + trailing)


def merge_patches(grid):
    row_count, lon_count, features = grid.shape
    view = grid.reshape(row_count // 2, 2, lon_count // 2, 2, features)
    view = view.transpose(0, 2, 1, 3, 4)
    return view.reshape(row_count // 2, lon_count // 2, 4, features)


def split_patches(patches):
    half_rows, half_lon, _, features = patches.shape
    view = patches.reshape(half_rows, half_lon, 2, 2, features).transpose(0, 2, 1, 3, 4)
    return view.reshape(half_rows * 2, half_lon * 2, features)


def feature_sums(first, second):
    return lax.psum((first, second), "mp")


def local_sums(first, second):
    return (first, second)


def group_sum(term):
    return lax.psum(term.astype(jnp.bfloat16), "mp").astype(jnp.float32)


def norm_forward(values, gain, axes, count, reducer):
    first, second = reducer(
        jnp.sum(values, axis=axes, keepdims=True),
        jnp.sum(values * values, axis=axes, keepdims=True),
    )
    center = first / count
    scale_inv = lax.rsqrt(second / count - center * center + EPSILON)
    unit = (values - center) * scale_inv
    return (unit * gain, unit, scale_inv)


def norm_backward(grad, gain, unit, scale_inv, axes, count, reducer):
    scaled = grad * gain
    first, second = reducer(
        jnp.sum(scaled, axis=axes, keepdims=True), jnp.sum(scaled * unit, axis=axes, keepdims=True)
    )
    return scale_inv * (scaled - first / count - unit * (second / count))


def attend(packed, labels):
    allow = labels[:, :, None] == labels[:, None, :]
    query = packed[:, :, 0]
    keys = packed[:, :, 1]
    values = packed[:, :, 2]
    factor = packed.shape[-1] ** (-0.5)
    scores = jnp.einsum("wqhe,wkhe->whqk", query, keys, preferred_element_type=jnp.float32) * factor
    scores = jnp.where(allow[:, None], scores, MASKED)
    highest = jnp.max(scores, axis=-1, keepdims=True)
    weights = jnp.exp(scores - highest)
    probs = weights / jnp.sum(weights, axis=-1, keepdims=True)
    context = jnp.einsum(
        "whqk,wkhe->wqhe", probs.astype(jnp.bfloat16), values, preferred_element_type=jnp.float32
    )
    return (context.astype(jnp.bfloat16), probs)


def attend_back(packed, probs, grad_context):
    query = packed[:, :, 0]
    keys = packed[:, :, 1]
    values = packed[:, :, 2]
    factor = packed.shape[-1] ** (-0.5)
    grad_probs = jnp.einsum(
        "wqhe,wkhe->whqk", grad_context, values, preferred_element_type=jnp.float32
    )
    grad_values = jnp.einsum(
        "whqk,wqhe->wkhe",
        probs.astype(jnp.bfloat16),
        grad_context,
        preferred_element_type=jnp.float32,
    ).astype(jnp.bfloat16)
    grad_scores = (
        probs * (grad_probs - jnp.sum(grad_probs * probs, axis=-1, keepdims=True)) * factor
    )
    grad_scores = grad_scores.astype(jnp.bfloat16)
    grad_query = jnp.einsum(
        "whqk,wkhe->wqhe", grad_scores, keys, preferred_element_type=jnp.float32
    ).astype(jnp.bfloat16)
    grad_keys = jnp.einsum(
        "whqk,wqhe->wkhe", grad_scores, query, preferred_element_type=jnp.float32
    ).astype(jnp.bfloat16)
    return jnp.stack([grad_query, grad_keys, grad_values], axis=2)


def shards(
    fields,
    first_gain,
    qkv_weight,
    proj_weight,
    merge_gain,
    merge_weight,
    mlp_gain,
    up_weight,
    down_weight,
    expand_weight,
    lat_shift,
    lon_shift,
    cotangent,
):
    lat_offset = lat_shift[0]
    lon_offset = lon_shift[0]
    row_count = fields.shape[0]
    lon_count = fields.shape[1]
    width_one = fields.shape[2] * lax.axis_size("mp")
    width_two = merge_weight.shape[2]
    local_width = qkv_weight.shape[2]
    heads_local = local_width // HDIM
    band_count = row_count // WIN_H
    column_count = lon_count // WIN_W
    margin = WIN_H - 1
    band_start = lax.axis_index("lat") * row_count
    total_rows = row_count * lax.axis_size("lat")
    row_index = band_start + jnp.arange(row_count, dtype=jnp.int32)
    region = (row_index >= jnp.int32(total_rows) - lat_offset).astype(jnp.int32)
    region_grid = jnp.broadcast_to(region[:, None], (row_count, lon_count))

    def into_frame(values, incoming):
        joined = jnp.concatenate([values, incoming], axis=0)
        framed_rows = lax.dynamic_slice_in_dim(joined, lat_offset, row_count, 0)
        return jnp.roll(framed_rows, -lon_offset, axis=1)

    def out_of_frame(values, incoming):
        joined = jnp.concatenate([incoming, values], axis=0)
        start = jnp.int32(incoming.shape[0]) - lat_offset
        framed_rows = lax.dynamic_slice_in_dim(joined, start, row_count, 0)
        return jnp.roll(framed_rows, lon_offset, axis=1)

    def head_gather(values):
        return lax.all_gather(values, "mp", axis=2, tiled=True)

    def head_scatter(partial_value):
        return lax.psum_scatter(partial_value, "mp", scatter_dimension=2, tiled=True).astype(
            jnp.float32
        )

    def frame_in(values):
        whole = head_gather(values)
        incoming = passed_along(whole[:margin], "lat", -1)
        return into_frame(whole, incoming)

    def frame_out(partial_value, keep_float):
        rounded = partial_value.astype(jnp.bfloat16)
        incoming = passed_along(rounded[-margin:], "lat", 1)
        shares = head_scatter(out_of_frame(rounded, incoming))
        if keep_float:
            return shares
        return shares.astype(jnp.bfloat16)

    fields_wide = fields.astype(jnp.float32)
    normed, unit_one, inv_one = norm_forward(fields_wide, first_gain, (2,), width_one, feature_sums)
    framed = frame_in(normed.astype(jnp.bfloat16))
    packed = jnp.einsum(
        "rld,dce->rlce", framed, qkv_weight, preferred_element_type=jnp.float32
    ).astype(jnp.bfloat16)
    windows = to_windows(packed.reshape(row_count, lon_count, 3, heads_local, HDIM))
    windows = windows.reshape((band_count * column_count,) + windows.shape[2:])
    label_windows = to_windows(region_grid).reshape(band_count * column_count, WIN_H * WIN_W)
    context_win, probs = attend(windows, label_windows)
    context_grid = from_windows(
        context_win.reshape((band_count, column_count) + context_win.shape[1:])
    )
    context_flat = context_grid.reshape(row_count, lon_count, local_width)
    proj_partial = jnp.einsum(
        "rle,oe->rlo", context_flat, proj_weight, preferred_element_type=jnp.float32
    )
    attention = frame_out(proj_partial, False)
    hidden = (fields_wide + attention.astype(jnp.float32)).astype(jnp.bfloat16)
    patches = merge_patches(hidden)
    normed_two, unit_two, inv_two = norm_forward(
        patches.astype(jnp.float32), merge_gain, (2, 3), 4 * width_one, feature_sums
    )
    patch_norm = normed_two.astype(jnp.bfloat16)
    merged = group_sum(
        jnp.einsum("abkd,kde->abe", patch_norm, merge_weight, preferred_element_type=jnp.float32)
    ).astype(jnp.bfloat16)
    merged_wide = merged.astype(jnp.float32)
    normed_three, unit_three, inv_three = norm_forward(
        merged_wide, mlp_gain, (2,), width_two, local_sums
    )
    mlp_in = normed_three.astype(jnp.bfloat16)
    hidden_up = jnp.einsum("abe,ef->abf", mlp_in, up_weight, preferred_element_type=jnp.float32)
    activated = jax.nn.gelu(hidden_up).astype(jnp.bfloat16)
    mlp_out = group_sum(
        jnp.einsum("abf,ef->abe", activated, down_weight, preferred_element_type=jnp.float32)
    )
    bottom = (merged_wide + mlp_out).astype(jnp.bfloat16)
    expanded = jnp.einsum(
        "abo,okd->abkd", bottom, expand_weight, preferred_element_type=jnp.float32
    )
    decoded = (hidden.astype(jnp.float32) + split_patches(expanded)).astype(jnp.bfloat16)
    cot_patches = merge_patches(cotangent)
    grad_bottom = group_sum(
        jnp.einsum("abkd,okd->abo", cot_patches, expand_weight, preferred_element_type=jnp.float32)
    )
    bottom_grad = grad_bottom.astype(jnp.bfloat16)
    grad_act = jnp.einsum(
        "abo,of->abf", bottom_grad, down_weight, preferred_element_type=jnp.float32
    )
    gelu_back = jax.vjp(jax.nn.gelu, hidden_up)[1]
    grad_pre = gelu_back(grad_act)[0].astype(jnp.bfloat16)
    down_local = jnp.einsum(
        "abo,abf->of", bottom_grad, activated, preferred_element_type=jnp.float32
    )
    up_local = jnp.einsum("abe,abf->ef", mlp_in, grad_pre, preferred_element_type=jnp.float32)
    grad_mlp_in = group_sum(
        jnp.einsum("abf,ef->abe", grad_pre, up_weight, preferred_element_type=jnp.float32)
    )
    grad_merged = grad_bottom + norm_backward(
        grad_mlp_in, mlp_gain, unit_three, inv_three, (2,), width_two, local_sums
    )
    grad_patch_norm = jnp.einsum(
        "abe,kde->abkd",
        grad_merged.astype(jnp.bfloat16),
        merge_weight,
        preferred_element_type=jnp.float32,
    )
    grad_patches = norm_backward(
        grad_patch_norm, merge_gain, unit_two, inv_two, (2, 3), 4 * width_one, feature_sums
    )
    grad_hidden = cotangent.astype(jnp.float32) + split_patches(grad_patches)
    grad_framed = frame_in(grad_hidden.astype(jnp.bfloat16))
    grad_context = jnp.einsum(
        "rlo,oe->rle", grad_framed, proj_weight, preferred_element_type=jnp.float32
    ).astype(jnp.bfloat16)
    proj_local = jnp.einsum(
        "rlo,rle->oe", grad_framed, context_flat, preferred_element_type=jnp.float32
    )
    grad_ctx_win = to_windows(grad_context.reshape(row_count, lon_count, heads_local, HDIM))
    grad_ctx_win = grad_ctx_win.reshape((band_count * column_count,) + grad_ctx_win.shape[2:])
    grad_win = attend_back(windows, probs, grad_ctx_win)
    grad_packed = from_windows(grad_win.reshape((band_count, column_count) + grad_win.shape[1:]))
    grad_packed = grad_packed.reshape(row_count, lon_count, 3, local_width)
    qkv_local = jnp.einsum("rld,rlce->dce", framed, grad_packed, preferred_element_type=jnp.float32)
    grad_norm_part = jnp.einsum(
        "rlce,dce->rld", grad_packed, qkv_weight, preferred_element_type=jnp.float32
    )
    grad_normed = frame_out(grad_norm_part, True)
    grad_input = grad_hidden + norm_backward(
        grad_normed, first_gain, unit_one, inv_one, (2,), width_one, feature_sums
    )
    grad_qkv, grad_proj, grad_up, grad_down = (
        lax.psum_scatter(
            qkv_local.astype(jnp.bfloat16), "lat", scatter_dimension=0, tiled=True
        ).astype(jnp.float32),
        lax.psum_scatter(
            proj_local.astype(jnp.bfloat16), "lat", scatter_dimension=0, tiled=True
        ).astype(jnp.float32),
        lax.psum_scatter(
            up_local.astype(jnp.bfloat16), "lat", scatter_dimension=0, tiled=True
        ).astype(jnp.float32),
        lax.psum_scatter(
            down_local.astype(jnp.bfloat16), "lat", scatter_dimension=0, tiled=True
        ).astype(jnp.float32),
    )
    return (decoded, grad_input, grad_qkv, grad_proj, grad_up, grad_down)


def solution(mesh):
    return jax.shard_map(
        shards,
        mesh=mesh,
        in_specs=(
            P("lat", None, "mp"),
            P("mp"),
            P(None, None, "mp"),
            P(None, "mp"),
            P(None, "mp"),
            P(None, "mp", None),
            P(),
            P(None, "mp"),
            P(None, "mp"),
            P(None, None, "mp"),
            P(),
            P(),
            P("lat", None, "mp"),
        ),
        out_specs=(
            P("lat", None, "mp"),
            P("lat", None, "mp"),
            P("lat", None, "mp"),
            P("lat", "mp"),
            P("lat", "mp"),
            P("lat", "mp"),
        ),
        check_vma=False,
    )
```

profile of v0, /device:TPU:1, one launch (start us, length us, event | category | flops | bytes accessed | tf_op | source)
XLA Modules:
  0.0 1284.9 jit_solution(10820817699267209669)
XLA Ops:
  9.9 36.8 %all-reduce.3 = (f32[12,288,1]{1,0,2:T(8,128)S(1)}, f32[12,288,1]{1,0,2:T(8,128)S(1)}) all-reduce(f32[12,288,1]{1,0,2:T(8,128)S(1)} %bitcast.227, f32[12,288,1]{1,0,2:T(8,128)S(1)} %bitcast.226), channel_id=1, replica_groups=mesh['lat'=16,'mp'=8] {'mp'}, use_global_device_ids=true, to_apply=%region_3.0 | all-reduce | flops 6912 | bytes 55296 | tf_op jit(solution)/shard_map/psum | solution.py:51
  49.0 79.6 %all-gather.3.cloned.1.call-done = bf16[12,288,512]{1,2,0:T(8,128)(2,1)} async-done(((bf16[12,288,64]{1,2,0:T(8,128)(2,1)}), bf16[12,288,512]{1,2,0:T(8,128)(2,1)}) %all-gather.3.cloned.1.call-update) | async-done | bytes 3538960 | tf_op jit(solution)/shard_map/all_gather | solution.py:169
  128.6 6.3 copy.144
  141.9 14.9 %collective-permute-done = bf16[5,288,512]{2,1,0:T(8,128)(2,1)S(1)} collective-permute-done((bf16[5,288,512]{2,1,0:T(8,128)(2,1)}, bf16[5,288,512]{2,1,0:T(8,128)(2,1)S(1)}, u32[]{:S(2)}, u32[]{:S(2)}) %collective-permute-start) | collective-permute-done | bytes 1474592 | tf_op jit(solution)/shard_map/ppermute | solution.py:18
  169.5 5.6 reshape_reshape.20
  185.5 4.2 fusion.135
  201.7 16.6 %collective-permute-done.1 = bf16[5,288,512]{2,1,0:T(8,128)(2,1)S(1)} collective-permute-done((bf16[5,288,512]{2,1,0:T(8,128)(2,1)}, bf16[5,288,512]{2,1,0:T(8,128)(2,1)S(1)}, u32[]{:S(2)}, u32[]{:S(2)}) %collective-permute-start.1) | collective-permute-done | bytes 1474592 | tf_op jit(solution)/shard_map/ppermute | solution.py:18
  220.6 4.6 fusion.20
  225.2 8.5 copy.156
  240.2 93.1 %reduce-scatter.7.cloned.1.call-done = bf16[12,288,64]{1,0,2:T(8,128)(2,1)} async-done(((bf16[12,288,512]{1,0,2:T(8,128)(2,1)}), bf16[12,288,64]{1,0,2:T(8,128)(2,1)}) %reduce-scatter.7.cloned.1.call-update) | async-done | bytes 442384 | tf_op jit(solution)/shard_map/reduce_scatter | solution.py:172
  338.2 5.0 fusion.132
  347.2 30.2 %all-reduce.2 = (f32[6,144,1,1]{1,0,3,2:T(8,128)S(1)}, f32[6,144,1,1]{1,0,3,2:T(8,128)S(1)}) all-reduce(f32[6,144,1,1]{1,0,3,2:T(8,128)S(1)} %bitcast.229, f32[6,144,1,1]{1,0,3,2:T(8,128)S(1)} %bitcast.228), channel_id=1, replica_groups=mesh['lat'=16,'mp'=8] {'mp'}, use_global_device_ids=true, to_apply=%region_10.12 | all-reduce | flops 1728 | bytes 13824 | tf_op jit(solution)/shard_map/psum | solution.py:51
  381.1 168.0 %all-reduce.11.cloned.1.call-done = (bf16[6,144,1024]{2,1,0:T(8,128)(2,1)}, bf16[6,144,1024]{2,1,0:T(8,128)(2,1)}) async-done(((bf16[6,144,1024]{2,1,0:T(8,128)(2,1)}, bf16[6,144,1024]{2,1,0:T(8,128)(2,1)}), (bf16[6,144,1024]{2,1,0:T(8,128)(2,1)}, bf16[6,144,1024]{2,1,0:T(8,128)(2,1)})) %all-reduce.11.cloned.1.call-update) | async-done | bytes 3538960 | tf_op jit(solution)/shard_map/psum | solution.py:59
  561.5 164.7 %all-reduce.9.cloned.1.call-done = (bf16[6,144,1024]{2,1,0:T(8,128)(2,1)}, bf16[6,144,1024]{2,1,0:T(8,128)(2,1)}) async-done(((bf16[6,144,1024]{2,1,0:T(8,128)(2,1)}, bf16[6,144,1024]{2,1,0:T(8,128)(2,1)}), (bf16[6,144,1024]{2,1,0:T(8,128)(2,1)}, bf16[6,144,1024]{2,1,0:T(8,128)(2,1)})) %all-reduce.9.cloned.1.call-update) | async-done | bytes 3538960 | tf_op jit(solution)/shard_map/psum | solution.py:59
  729.6 5.4 fusion.133
  734.9 33.3 %all-reduce.1 = (f32[6,144,1,1]{1,0,3,2:T(8,128)S(1)}, f32[6,144,1,1]{1,0,3,2:T(8,128)S(1)}) all-reduce(f32[6,144,1,1]{1,0,3,2:T(8,128)S(1)} %bitcast.231, f32[6,144,1,1]{1,0,3,2:T(8,128)S(1)} %bitcast.230), channel_id=1, replica_groups=mesh['lat'=16,'mp'=8] {'mp'}, use_global_device_ids=true, to_apply=%region_22.24 | all-reduce | flops 1728 | bytes 13824 | tf_op jit(solution)/shard_map/psum | solution.py:51
  782.7 75.7 %all-gather.5.cloned.1.call-done = bf16[12,288,512]{1,2,0:T(8,128)(2,1)} async-done(((bf16[12,288,64]{1,2,0:T(8,128)(2,1)}), bf16[12,288,512]{1,2,0:T(8,128)(2,1)}) %all-gather.5.cloned.1.call-update) | async-done | bytes 3538960 | tf_op jit(solution)/shard_map/all_gather | solution.py:169
  858.4 6.3 copy.166
  872.7 15.8 %collective-permute-done.2 = bf16[5,288,512]{2,1,0:T(8,128)(2,1)} collective-permute-done((bf16[5,288,512]{2,1,0:T(8,128)(2,1)}, bf16[5,288,512]{2,1,0:T(8,128)(2,1)}, u32[]{:S(2)}, u32[]{:S(2)}) %collective-permute-start.2) | collective-permute-done | bytes 1474592 | tf_op jit(solution)/shard_map/ppermute | solution.py:18
  908.9 5.1 fusion.67
  916.2 5.1 fusion.70
  928.5 5.7 reshape_reshape.25
  944.9 6.7 fusion.75
  951.8 7.1 collective-permute-done.3
  961.7 4.5 fusion.18
  966.2 8.5 copy.179
  976.3 27.6 %reduce-scatter.17.cloned.1.call-done = bf16[64,512]{1,0:T(8,128)(2,1)} async-done(((bf16[1024,512]{1,0:T(8,128)(2,1)}), bf16[64,512]{1,0:T(8,128)(2,1)}) %reduce-scatter.17.cloned.1.call-update) | async-done | bytes 65552 | tf_op jit(solution)/shard_map/reduce_scatter | solution.py:291
  1013.4 50.5 %reduce-scatter.13.cloned.1.call-done = bf16[32,64]{1,0:T(8,128)(2,1)} async-done(((bf16[512,64]{1,0:T(8,128)(2,1)}), bf16[32,64]{1,0:T(8,128)(2,1)}) %reduce-scatter.13.cloned.1.call-update) | async-done | bytes 4112 | tf_op jit(solution)/shard_map/reduce_scatter | solution.py:285
  1065.2 60.6 %reduce-scatter.11.cloned.1.call-done = bf16[32,3,64]{2,0,1:T(8,128)(2,1)} async-done(((bf16[512,3,64]{2,0,1:T(8,128)(2,1)}), bf16[32,3,64]{2,0,1:T(8,128)(2,1)}) %reduce-scatter.11.cloned.1.call-update) | async-done | bytes 12304 | tf_op jit(solution)/shard_map/reduce_scatter | solution.py:282
  1127.2 103.8 %reduce-scatter.9.cloned.1.call-done = bf16[12,288,64]{1,0,2:T(8,128)(2,1)} async-done(((bf16[12,288,512]{1,0,2:T(8,128)(2,1)}), bf16[12,288,64]{1,0,2:T(8,128)(2,1)}) %reduce-scatter.9.cloned.1.call-update) | async-done | bytes 442384 | tf_op jit(solution)/shard_map/reduce_scatter | solution.py:172
  1236.9 31.0 %all-reduce = (f32[12,288,1]{1,0,2:T(8,128)S(1)}, f32[12,288,1]{1,0,2:T(8,128)S(1)}) all-reduce(f32[12,288,1]{1,0,2:T(8,128)S(1)} %bitcast.225, f32[12,288,1]{1,0,2:T(8,128)S(1)} %bitcast.224), channel_id=1, replica_groups=mesh['lat'=16,'mp'=8] {'mp'}, use_global_device_ids=true, to_apply=%region_28.30 | all-reduce | flops 6912 | bytes 55296 | tf_op jit(solution)/shard_map/psum | solution.py:51
  1267.9 5.5 fusion.39
  (166 shorter events, 172.6 us)
Async XLA Ops:
  7.2 546.5 %copy-start = (bf16[1024,512]{1,0:T(8,128)(2,1)S(1)}, bf16[1024,512]{1,0:T(8,128)(2,1)}, u32[]{:S(2)}) copy-start(bf16[1024,512]{1,0:T(8,128)(2,1)} %param.23) | copy-start | bytes 3145732
  7.2 39.5 %copy-start.17 = (f32[64]{0:T(128)S(1)}, f32[64]{0:T(128)}, u32[]{:S(2)}) copy-start(f32[64]{0:T(128)} %param.16) | copy-start | bytes 772
  7.2 121.5 %all-gather.3.cloned.1.call-start = ((), (), s32[]{:S(2)}) async-start(), calls=%async_computation.6 | async-start | bytes 5308416 | tf_op jit(solution)/shard_map/all_gather | solution.py:169
  49.0 284.3 %reduce-scatter.7.cloned.1.call-start = ((), (), s32[]{:S(2)}) async-start(), calls=%async_computation.7 | async-start | bytes 7077888 | tf_op jit(solution)/shard_map/reduce_scatter | solution.py:172
  137.6 19.3 %collective-permute-start = (bf16[5,288,512]{2,1,0:T(8,128)(2,1)}, bf16[5,288,512]{2,1,0:T(8,128)(2,1)S(1)}, u32[]{:S(2)}, u32[]{:S(2)}) collective-permute-start(bf16[5,288,512]{2,1,0:T(8,128)(2,1)} %slice.31), channel_id=1, source_target_pairs={{0,120},{8,0},{16,8},{24,16},{32,24},{40,32},{48,40},{56,48},{64,5... | collective-permute-start | bytes 4423688 | tf_op jit(solution)/shard_map/ppermute | solution.py:18
  141.9 19.2 %copy-start.25 = (bf16[512,3,64]{0,2,1:T(8,128)(2,1)S(1)}, bf16[512,3,64]{0,2,1:T(8,128)(2,1)}, u32[]{:S(2)}) copy-start(bf16[512,3,64]{0,2,1:T(8,128)(2,1)} %param.17) | copy-start | bytes 589828
  185.5 4.3 copy-start.14
  201.2 17.1 %collective-permute-start.1 = (bf16[5,288,512]{2,1,0:T(8,128)(2,1)}, bf16[5,288,512]{2,1,0:T(8,128)(2,1)S(1)}, u32[]{:S(2)}, u32[]{:S(2)}) collective-permute-start(bf16[5,288,512]{2,1,0:T(8,128)(2,1)} %slice.35), channel_id=1, source_target_pairs={{0,8},{8,16},{16,24},{24,32},{32,40},{40,48},{48,56},{56,64},{64,7... | collective-permute-start | bytes 4423688 | tf_op jit(solution)/shard_map/ppermute | solution.py:18
  233.7 315.4 %all-reduce.11.cloned.1.call-start = ((), (), s32[]{:S(2)}) async-start(), calls=%async_computation.15 | async-start | bytes 7077888 | tf_op jit(solution)/shard_map/psum | solution.py:59
  343.2 34.2 %copy-start.23 = (bf16[4,64,1024]{2,1,0:T(8,128)(2,1)S(1)}, bf16[4,64,1024]{2,1,0:T(8,128)(2,1)}, u32[]{:S(2)}) copy-start(bf16[4,64,1024]{2,1,0:T(8,128)(2,1)} %param.20) | copy-start | bytes 1572868
  343.3 34.2 %copy-start.27 = (f32[4,64]{1,0:T(4,128)S(1)}, f32[4,64]{1,0:T(4,128)}, u32[]{:S(2)}) copy-start(f32[4,64]{1,0:T(4,128)} %param.19) | copy-start | bytes 3076
  380.9 170.4 %copy-start.19 = (f32[1024]{0:T(1024)S(1)}, f32[1024]{0:T(1024)}, u32[]{:S(2)}) copy-start(f32[1024]{0:T(1024)} %param.21) | copy-start | bytes 12292
  380.9 345.3 %all-reduce.9.cloned.1.call-start = ((), (), s32[]{:S(2)}) async-start(), calls=%async_computation.14 | async-start | bytes 7077888 | tf_op jit(solution)/shard_map/psum | solution.py:59
  556.2 2.9 copy-start.22
  561.5 296.9 %all-gather.5.cloned.1.call-start = ((), (), s32[]{:S(2)}) async-start(), calls=%async_computation.8 | async-start | bytes 5308416 | tf_op jit(solution)/shard_map/all_gather | solution.py:169
  726.2 3.4 copy-start.7
  726.2 3.4 copy-start.8
  778.4 196.3 %reduce-scatter.15.cloned.1.call-start = ((), (), s32[]{:S(2)}) async-start(), calls=%async_computation.12 | async-start | bytes 1114112 | tf_op jit(solution)/shard_map/reduce_scatter | solution.py:288
  782.7 221.3 %reduce-scatter.17.cloned.1.call-start = ((), (), s32[]{:S(2)}) async-start(), calls=%async_computation.13 | async-start | bytes 1114112 | tf_op jit(solution)/shard_map/reduce_scatter | solution.py:291
  864.6 4.1 copy-start.21
  867.5 21.1 %collective-permute-start.2 = (bf16[5,288,512]{2,1,0:T(8,128)(2,1)}, bf16[5,288,512]{2,1,0:T(8,128)(2,1)}, u32[]{:S(2)}, u32[]{:S(2)}) collective-permute-start(bf16[5,288,512]{2,1,0:T(8,128)(2,1)} %slice.36), channel_id=1, source_target_pairs={{0,120},{8,0},{16,8},{24,16},{32,24},{40,32},{48,40},{56,48},{64,5... | collective-permute-start | bytes 4423688 | tf_op jit(solution)/shard_map/ppermute | solution.py:18
  872.7 191.2 %reduce-scatter.13.cloned.1.call-start = ((), (), s32[]{:S(2)}) async-start(), calls=%async_computation.11 | async-start | bytes 139264 | tf_op jit(solution)/shard_map/reduce_scatter | solution.py:285
  928.5 5.7 copy-start.26
  934.2 6.6 copy-start.12
  940.4 18.6 %collective-permute-start.3 = (bf16[5,288,512]{2,1,0:T(8,128)(2,1)}, bf16[5,288,512]{2,1,0:T(8,128)(2,1)}, u32[]{:S(2)}, u32[]{:S(2)}) collective-permute-start(bf16[5,288,512]{2,1,0:T(8,128)(2,1)} %slice.37), channel_id=1, source_target_pairs={{0,8},{8,16},{16,24},{24,32},{32,40},{40,48},{48,56},{56,64},{64,7... | collective-permute-start | bytes 4423688 | tf_op jit(solution)/shard_map/ppermute | solution.py:18
  944.9 181.0 %reduce-scatter.11.cloned.1.call-start = ((), (), s32[]{:S(2)}) async-start(), calls=%async_computation.10 | async-start | bytes 417792 | tf_op jit(solution)/shard_map/reduce_scatter | solution.py:282
  951.6 279.4 %reduce-scatter.9.cloned.1.call-start = ((), (), s32[]{:S(2)}) async-start(), calls=%async_computation.9 | async-start | bytes 7077888 | tf_op jit(solution)/shard_map/reduce_scatter | solution.py:172
  974.7 30.7 %copy-start.24 = (bf16[1024,4,64]{0,2,1:T(8,128)(2,1)S(1)}, bf16[1024,4,64]{0,2,1:T(8,128)(2,1)}, u32[]{:S(2)}) copy-start(bf16[1024,4,64]{0,2,1:T(8,128)(2,1)} %param.24) | copy-start | bytes 1572868
  1009.6 223.7 %copy-start.18 = (f32[64]{0:T(128)S(1)}, f32[64]{0:T(128)}, u32[]{:S(2)}) copy-start(f32[64]{0:T(128)} %param.16) | copy-start | bytes 772
  1127.2 140.7 %copy-start.4 = (bf16[12,288,64]{2,1,0:T(8,128)(2,1)S(1)}, bf16[12,288,64]{2,1,0:T(8,128)(2,1)}, u32[]{:S(2)}) copy-start(bf16[12,288,64]{2,1,0:T(8,128)(2,1)} %copy.157) | copy-start | bytes 1327108
  1273.4 3.3 copy-start.9
  1273.4 4.5 copy-start.1
  (13 other events, 25.0 us)
Sparse Core Ops, SparseCore 0:
  49.1 79.4 all-gather.2
  233.8 99.4 reduce-scatter.6
  381.0 168.0 all-reduce.10
  561.6 164.5 all-reduce.8
  778.6 79.7 all-gather.4
  860.7 70.1 reduce-scatter.14
  933.3 70.5 reduce-scatter.16
  1006.9 56.9 reduce-scatter.12
  1066.8 58.9 reduce-scatter.10
  1130.1 100.8 reduce-scatter.8
where the time goes:
time: 1300 us; the launch traced here: 1280 us
  waiting for transfers between devices  878 us (68%)
  blocking collectives  131 us (10%)
  local copies, waits for them, and re-layouts  120 us (9%)
  matrix products  79.3 us (6%)
  other arithmetic  55.6 us (4%)
  between operations  16.2 us (1%)
    psum x2, waiting for transfers between devices, group_sum(): return lax.psum(term.astype(jnp.bfloat16), 'mp').astype(jnp.float32)  333 us
    reduce_scatter x2, waiting for transfers between devices, head_scatter(): lax.psum_scatter(partial_value, 'mp', scatter_dimension=2, tiled=True)  197 us
    all_gather x2, waiting for transfers between devices, head_gather(): return lax.all_gather(values, 'mp', axis=2, tiled=True)  155 us
    psum x4, blocking collectives, feature_sums(): return lax.psum((first, second), 'mp')  131 us
    reduce_scatter x1, waiting for transfers between devices, shards(): lax.psum_scatter(qkv_local.astype(jnp.bfloat16), 'lat', scatter_dimension...  60.6 us
    ppermute x4, waiting for transfers between devices, passed_along(): return lax.ppermute(value, axis, pairs)  54.5 us
    reduce_scatter x1, waiting for transfers between devices, shards(): lax.psum_scatter(proj_local.astype(jnp.bfloat16), 'lat', scatter_dimensio...  50.5 us
    reduce_scatter x1, waiting for transfers between devices, shards(): lax.psum_scatter(down_local.astype(jnp.bfloat16), 'lat', scatter_dimensio...  27.6 us
  transfers between devices with their start and end apart: 14, of which 13 were waited for; matrix products, arithmetic and copies ran while one was open for 9% of the time, Pallas kernels for 0%

commit v1 on v0

v1 whole, which is shorter than its diff:
```python
import jax
import jax.numpy as jnp
from jax import lax
from jax.experimental import pallas as pl
from jax.experimental.pallas import tpu as pltpu
from jax.sharding import PartitionSpec as P

WIN_H = 6
WIN_W = 12
HDIM = 64
EPSILON = 1e-05
MASKED = -1e30
BF16 = jnp.bfloat16
F32 = jnp.float32


def exchange(collective, inputs, outputs, moves):
    n_lat, n_mp = lax.axis_size("lat"), lax.axis_size("mp")
    steps = sorted({(move[4] % n_lat, move[5] % n_mp) for move in moves} - {(0, 0)})

    def body(*refs):
        sources = refs[: len(inputs)]
        landings = refs[len(inputs) : len(inputs) + len(outputs)]
        send, receive = refs[-2:]
        here = {"lat": lax.axis_index("lat"), "mp": lax.axis_index("mp")}
        barrier = pltpu.get_barrier_semaphore()
        for down, right in steps:
            pl.semaphore_signal(
                barrier,
                inc=1,
                device_id=(
                    lax.rem(here["lat"] + n_lat - down, n_lat),
                    lax.rem(here["mp"] + n_mp - right, n_mp),
                ),
                device_id_type=pl.DeviceIdType.MESH,
            )
        pl.semaphore_wait(barrier, len(steps))
        copies = []
        for index, (source, source_slot, landing, landing_slot, down, right) in enumerate(moves):
            down, right = down % n_lat, right % n_mp
            target = {
                "lat": lax.rem(here["lat"] + down, n_lat),
                "mp": lax.rem(here["mp"] + right, n_mp),
            }
            source_ref = sources[source]
            if source_slot is not None:
                source_ref = source_ref.at[target[source_slot]]
            landing_ref = landings[landing]
            if landing_slot is not None:
                landing_ref = landing_ref.at[here[landing_slot]]
            if (down, right) == (0, 0):
                copy = pltpu.make_async_copy(source_ref, landing_ref, receive.at[index])
            else:
                copy = pltpu.make_async_remote_copy(
                    src_ref=source_ref,
                    dst_ref=landing_ref,
                    send_sem=send.at[index],
                    recv_sem=receive.at[index],
                    device_id=(target["lat"], target["mp"]),
                    device_id_type=pl.DeviceIdType.MESH,
                )
            copy.start()
            copies.append(copy)
        for copy in copies:
            copy.wait()

    return pl.pallas_call(
        body,
        out_shape=[jax.ShapeDtypeStruct(shape, dtype) for shape, dtype in outputs],
        in_specs=[pl.BlockSpec(memory_space=pl.ANY)] * len(inputs),
        out_specs=[pl.BlockSpec(memory_space=pl.ANY)] * len(outputs),
        scratch_shapes=[
            pltpu.SemaphoreType.DMA((len(moves),)),
            pltpu.SemaphoreType.DMA((len(moves),)),
        ],
        compiler_params=pltpu.CompilerParams(collective_id=collective, has_side_effects=True),
    )(*inputs)


def halves_beside(values):
    half = values.shape[-2] // 2
    return jnp.concatenate([values[..., :half, :], values[..., half:, :]], axis=-1)


def groups_joined(slabs):
    count, half, _ = slabs.shape
    view = slabs.reshape(count, half, 2, HDIM).transpose(2, 1, 0, 3)
    return view.reshape(2 * half, count * HDIM)


def to_windows(grid):
    row_count, lon_count = (grid.shape[0], grid.shape[1])
    trailing = grid.shape[2:]
    view = grid.reshape((row_count // WIN_H, WIN_H, lon_count // WIN_W, WIN_W) + trailing)
    view = jnp.swapaxes(view, 1, 2)
    return view.reshape(((row_count // WIN_H) * (lon_count // WIN_W), WIN_H * WIN_W) + trailing)


def from_windows(windows, bands, columns):
    trailing = windows.shape[2:]
    view = windows.reshape((bands, columns, WIN_H, WIN_W) + trailing)
    view = jnp.swapaxes(view, 1, 2)
    return view.reshape((bands * WIN_H, columns * WIN_W) + trailing)


def merge_patches(grid):
    row_count, lon_count, features = grid.shape
    view = grid.reshape(row_count // 2, 2, lon_count // 2, 2, features)
    view = view.transpose(0, 2, 1, 3, 4)
    return view.reshape(row_count * lon_count // 4, 4, features)


def split_patches(patches, row_count, lon_count):
    features = patches.shape[-1]
    view = patches.reshape(row_count // 2, lon_count // 2, 2, 2, features)
    return view.transpose(0, 2, 1, 3, 4).reshape(row_count, lon_count, features)


def norm_forward(values, gain, axes):
    center = jnp.mean(values, axis=axes, keepdims=True)
    second = jnp.mean(values * values, axis=axes, keepdims=True)
    scale_inv = lax.rsqrt(second - center * center + EPSILON)
    unit = (values - center) * scale_inv
    return (unit * gain, unit, scale_inv)


def norm_backward(grad, gain, unit, scale_inv, axes):
    scaled = grad * gain
    first = jnp.mean(scaled, axis=axes, keepdims=True)
    second = jnp.mean(scaled * unit, axis=axes, keepdims=True)
    return scale_inv * (scaled - first - unit * second)


def attend(packed, labels):
    allow = labels[:, :, None] == labels[:, None, :]
    query, keys, values = packed[..., 0, :], packed[..., 1, :], packed[..., 2, :]
    factor = packed.shape[-1] ** (-0.5)
    scores = jnp.einsum("wqhe,wkhe->whqk", query, keys, preferred_element_type=F32) * factor
    scores = jnp.where(allow[:, None], scores, MASKED)
    weights = jnp.exp(scores - jnp.max(scores, axis=-1, keepdims=True))
    probs = weights / jnp.sum(weights, axis=-1, keepdims=True)
    context = jnp.einsum("whqk,wkhe->wqhe", probs.astype(BF16), values, preferred_element_type=F32)
    return (context.astype(BF16), probs)


def attend_back(packed, probs, grad_context):
    query, keys, values = packed[..., 0, :], packed[..., 1, :], packed[..., 2, :]
    factor = packed.shape[-1] ** (-0.5)
    grad_probs = jnp.einsum("wqhe,wkhe->whqk", grad_context, values, preferred_element_type=F32)
    grad_values = jnp.einsum(
        "whqk,wqhe->wkhe", probs.astype(BF16), grad_context, preferred_element_type=F32
    ).astype(BF16)
    grad_scores = (
        probs * (grad_probs - jnp.sum(grad_probs * probs, axis=-1, keepdims=True)) * factor
    ).astype(BF16)
    grad_query = jnp.einsum(
        "whqk,wkhe->wqhe", grad_scores, keys, preferred_element_type=F32
    ).astype(BF16)
    grad_keys = jnp.einsum(
        "whqk,wqhe->wkhe", grad_scores, query, preferred_element_type=F32
    ).astype(BF16)
    return jnp.stack([grad_query, grad_keys, grad_values], axis=3)


def shards(
    fields,
    first_gain,
    qkv_weight,
    proj_weight,
    merge_gain,
    merge_weight,
    mlp_gain,
    up_weight,
    down_weight,
    expand_weight,
    lat_shift,
    lon_shift,
    cotangent,
):
    n_lat, n_mp = lax.axis_size("lat"), lax.axis_size("mp")
    lat_offset = lat_shift[0]
    lon_offset = lon_shift[0]
    rows, lon_count, group = fields.shape
    width = group * n_mp
    block = lon_count // n_mp
    wide = block + WIN_W
    tall = rows + WIN_H
    bands, columns = rows // WIN_H, block // WIN_W
    tokens = rows * block
    width_two = merge_weight.shape[2]
    span = up_weight.shape[1]
    merged_count = tokens // 4
    padded = -(-merged_count // 16) * 16
    others = range(n_mp)

    def column_blocks(values, extent):
        ring = jnp.concatenate([values, values[:, : extent - block]], axis=1)
        return jnp.stack(
            [ring[:, block * at : block * at + extent] for at in range(n_mp)], axis=0
        )

    field_blocks = column_blocks(fields, wide)
    body_slab = halves_beside(field_blocks.reshape(n_mp, rows * wide, group))
    cot_slab = halves_beside(column_blocks(cotangent, block).reshape(n_mp, tokens, group))
    slabs = jnp.concatenate([body_slab, cot_slab], axis=1)
    edge_slab = halves_beside(field_blocks[:, :WIN_H].reshape(n_mp, WIN_H * wide, group))
    weights = jnp.concatenate(
        [qkv_weight.reshape(width, 3 * group), proj_weight], axis=1
    )
    gains = jnp.pad(jnp.concatenate([first_gain[None], merge_gain], axis=0), ((0, 3), (0, 64)))
    merge_all = lax.all_gather(merge_weight, "mp", axis=1, tiled=True)
    expand_all = lax.all_gather(expand_weight, "mp", axis=0)
    got, got_edge, weights_all, gains_all = exchange(
        1,
        [slabs, edge_slab, weights, gains],
        [
            (slabs.shape, BF16),
            (edge_slab.shape, BF16),
            ((n_mp,) + weights.shape, BF16),
            ((n_mp,) + gains.shape, F32),
        ],
        [(2, None, 2, "mp", 0, step) for step in others]
        + [(3, None, 3, "mp", 0, step) for step in others]
        + [(0, "mp", 0, "mp", 0, step) for step in others]
        + [(1, "mp", 1, "mp", -1, step) for step in others],
    )
    body_half = rows * wide // 2
    body = groups_joined(got[:, :body_half]).reshape(rows, wide, width)
    edge = groups_joined(got_edge).reshape(WIN_H, wide, width)
    cot = groups_joined(got[:, body_half:]).reshape(rows, block, width)
    first_all = gains_all[:, 0, :group].reshape(width)
    merge_gain_all = gains_all[:, 1:5, :group].transpose(1, 0, 2).reshape(4, width)
    qkv_all = weights_all[:, :, : 3 * group].reshape(n_mp, width, 3, group)
    proj_all = weights_all[:, :, 3 * group :]

    def into_frame(whole):
        return lax.dynamic_slice(
            whole, (lat_offset, lon_offset, jnp.int32(0)), (rows, block, width)
        )

    own_fields = body[:, :block].astype(F32)
    framed_fields = to_windows(into_frame(jnp.concatenate([body, edge], axis=0)))
    normed, unit_one, inv_one = norm_forward(framed_fields.astype(F32), first_all, (2,))
    framed = normed.astype(BF16)
    packed = jnp.einsum("wtd,mdce->wtmce", framed, qkv_all, preferred_element_type=F32).astype(BF16)
    row_index = lax.axis_index("lat") * rows + jnp.arange(rows, dtype=jnp.int32)
    region = (row_index >= jnp.int32(rows) * n_lat - lat_offset).astype(jnp.int32)
    labels = to_windows(jnp.broadcast_to(region[:, None], (rows, block)))
    context, probs = attend(packed, labels)
    attention_framed = jnp.einsum(
        "wtme,moe->wto", context, proj_all, preferred_element_type=F32
    ).astype(BF16)
    attention_grid = from_windows(attention_framed, bands, columns)
    from_above, from_left, from_corner = exchange(
        2,
        [
            attention_grid[-WIN_H:].reshape(WIN_H * block, width),
            attention_grid[:, -WIN_W:].reshape(rows * WIN_W, width),
            attention_grid[-WIN_H:, -WIN_W:].reshape(WIN_H * WIN_W, width),
        ],
        [
            ((WIN_H * block, width), BF16),
            ((rows * WIN_W, width), BF16),
            ((WIN_H * WIN_W, width), BF16),
        ],
        [(0, None, 0, None, 1, 0), (1, None, 1, None, 0, 1), (2, None, 2, None, 1, 1)],
    )
    top = jnp.concatenate(
        [from_corner.reshape(WIN_H, WIN_W, width), from_above.reshape(WIN_H, block, width)], axis=1
    )
    low = jnp.concatenate([from_left.reshape(rows, WIN_W, width), attention_grid], axis=1)
    attention = lax.dynamic_slice(
        jnp.concatenate([top, low], axis=0),
        (WIN_H - lat_offset, WIN_W - lon_offset, jnp.int32(0)),
        (rows, block, width),
    )
    hidden = merge_patches((own_fields + attention.astype(F32)).astype(BF16))
    hidden_wide = hidden.astype(F32)
    normed_two, unit_two, inv_two = norm_forward(hidden_wide, merge_gain_all, (1, 2))
    merged = jnp.einsum(
        "akd,kde->ae", normed_two.astype(BF16), merge_all, preferred_element_type=F32
    ).astype(BF16)
    merged_wide = merged.astype(F32)
    normed_three, unit_three, inv_three = norm_forward(merged_wide, mlp_gain, (1,))
    cot_patches = merge_patches(cot)
    grad_bottom = jnp.einsum(
        "akmd,mokd->ao",
        cot_patches.reshape(merged_count, 4, n_mp, group),
        expand_all,
        preferred_element_type=F32,
    )
    pair = jnp.concatenate([normed_three.astype(BF16), grad_bottom.astype(BF16)], axis=1)
    pair = jnp.pad(pair, ((0, padded - merged_count), (0, 0)))
    (pairs,) = exchange(
        3,
        [pair],
        [((n_mp,) + pair.shape, BF16)],
        [(0, None, 0, "mp", 0, step) for step in others],
    )
    pairs = pairs.reshape(n_mp * padded, 2 * width_two)
    mlp_in, bottom_grad = pairs[:, :width_two], pairs[:, width_two:]
    hidden_up = jnp.dot(mlp_in, up_weight, preferred_element_type=F32)
    activated = jax.nn.gelu(hidden_up).astype(BF16)
    grad_act = jnp.dot(bottom_grad, down_weight, preferred_element_type=F32)
    gelu_back = jax.vjp(jax.nn.gelu, hidden_up)[1]
    grad_pre = gelu_back(grad_act)[0].astype(BF16)
    terms = jnp.concatenate(
        [
            jnp.einsum("af,ef->ae", activated, down_weight, preferred_element_type=F32),
            jnp.einsum("af,ef->ae", grad_pre, up_weight, preferred_element_type=F32),
        ],
        axis=1,
    ).astype(BF16)
    (parts,) = exchange(
        4,
        [terms.reshape(n_mp, padded, 2 * width_two)],
        [((n_mp, padded, 2 * width_two), BF16)],
        [(0, "mp", 0, "mp", 0, step) for step in others],
    )
    down_local = jnp.einsum("ao,af->of", bottom_grad, activated, preferred_element_type=F32)
    up_local = jnp.einsum("ae,af->ef", mlp_in, grad_pre, preferred_element_type=F32)
    grad_up, grad_down = (
        lax.psum_scatter(part.astype(BF16), "lat", scatter_dimension=0, tiled=True).astype(F32)
        for part in (up_local, down_local)
    )
    totals = jnp.sum(parts[:, :merged_count].astype(F32), axis=0)
    bottom = (merged_wide + totals[:, :width_two]).astype(BF16)
    expanded = jnp.einsum("ao,mokd->akmd", bottom, expand_all, preferred_element_type=F32)
    decoded = (hidden_wide + expanded.reshape(merged_count, 4, width)).astype(BF16)
    grad_merged = grad_bottom + norm_backward(
        totals[:, width_two:], mlp_gain, unit_three, inv_three, (1,)
    )
    grad_patch_norm = jnp.einsum(
        "ae,kde->akd", grad_merged.astype(BF16), merge_all, preferred_element_type=F32
    )
    grad_patches = norm_backward(grad_patch_norm, merge_gain_all, unit_two, inv_two, (1, 2))
    grad_hidden = split_patches(
        (cot_patches.astype(F32) + grad_patches).astype(BF16), rows, block
    )

    def group_slabs(grid):
        count = grid.shape[0] * grid.shape[1]
        view = grid.reshape(count, n_mp, group).transpose(1, 0, 2)
        return halves_beside(view)

    decoded_slab = group_slabs(split_patches(decoded, rows, block))
    from_below, from_right, from_corner, decoded_got = exchange(
        5,
        [
            grad_hidden[:WIN_H].reshape(WIN_H * block, width),
            grad_hidden[:, :WIN_W].reshape(rows * WIN_W, width),
            grad_hidden[:WIN_H, :WIN_W].reshape(WIN_H * WIN_W, width),
            decoded_slab,
        ],
        [
            ((WIN_H * block, width), BF16),
            ((rows * WIN_W, width), BF16),
            ((WIN_H * WIN_W, width), BF16),
            (decoded_slab.shape, BF16),
        ],
        [(0, None, 0, None, -1, 0), (1, None, 1, None, 0, -1), (2, None, 2, None, -1, -1)]
        + [(3, "mp", 3, "mp", 0, step) for step in others],
    )

    def columns_joined(slabs, row_count):
        count = slabs.shape[0]
        view = jnp.concatenate([slabs[..., :group], slabs[..., group:]], axis=1)
        view = view.reshape(count, row_count, block, group).transpose(1, 0, 2, 3)
        return view.reshape(row_count, count * block, group)

    decoded_out = columns_joined(decoded_got, rows)
    high = jnp.concatenate([grad_hidden, from_right.reshape(rows, WIN_W, width)], axis=1)
    bottom_rows = jnp.concatenate(
        [from_below.reshape(WIN_H, block, width), from_corner.reshape(WIN_H, WIN_W, width)], axis=1
    )
    grad_framed = to_windows(into_frame(jnp.concatenate([high, bottom_rows], axis=0)))
    grad_context = jnp.einsum(
        "wto,moe->wtme", grad_framed, proj_all, preferred_element_type=F32
    ).astype(BF16)
    grad_proj_part = jnp.einsum("wto,wtme->moe", grad_framed, context, preferred_element_type=F32)
    grad_packed = attend_back(packed, probs, grad_context)
    grad_qkv_part = jnp.einsum("wtd,wtmce->mdce", framed, grad_packed, preferred_element_type=F32)
    grad_normed = jnp.einsum("wtmce,mdce->wtd", grad_packed, qkv_all, preferred_element_type=F32)
    grad_input_framed = grad_framed.astype(F32) + norm_backward(
        grad_normed, first_all, unit_one, inv_one, (2,)
    )
    grad_grid = from_windows(grad_input_framed.astype(BF16), bands, columns)
    grad_slab = group_slabs(grad_grid)
    grad_edge = jnp.pad(group_slabs(grad_grid[-WIN_H:]), ((0, 0), (0, 4), (0, 0)))
    weight_slab = jnp.concatenate(
        [grad_qkv_part.reshape(n_mp, width, 3 * group), grad_proj_part], axis=2
    ).astype(BF16)
    grad_got, edge_got, weight_got = exchange(
        6,
        [grad_slab, grad_edge, weight_slab],
        [(grad_slab.shape, BF16), (grad_edge.shape, BF16), (weight_slab.shape, BF16)],
        [(2, "mp", 2, "mp", 0, step) for step in others]
        + [(0, "mp", 0, "mp", 0, step) for step in others]
        + [(1, "mp", 1, "mp", 1, step) for step in others],
    )
    weight_sum = jnp.sum(weight_got.astype(F32), axis=0).astype(BF16)
    (lat_got,) = exchange(
        7,
        [weight_sum.reshape(n_lat, width // n_lat, 4 * group)],
        [((n_lat, width // n_lat, 4 * group), BF16)],
        [(0, "lat", 0, "lat", step, 0) for step in range(n_lat)],
    )
    weight_total = jnp.sum(lat_got.astype(F32), axis=0)
    grad_qkv = weight_total[:, : 3 * group].reshape(width // n_lat, 3, group)
    grad_proj = weight_total[:, 3 * group :]
    edge_half = WIN_H * block // 2
    grad_rows = jnp.concatenate(
        [columns_joined(edge_got[:, :edge_half], WIN_H), columns_joined(grad_got, rows)], axis=0
    )
    grad_rows = jnp.concatenate([grad_rows[:, -WIN_W:], grad_rows], axis=1)
    grad_input = lax.dynamic_slice(
        grad_rows,
        (WIN_H - lat_offset, WIN_W - lon_offset, jnp.int32(0)),
        (rows, lon_count, group),
    ).astype(F32)
    return (decoded_out, grad_input, grad_qkv, grad_proj, grad_up, grad_down)


def solution(mesh):
    return jax.shard_map(
        shards,
        mesh=mesh,
        in_specs=(
            P("lat", None, "mp"),
            P("mp"),
            P(None, None, "mp"),
            P(None, "mp"),
            P(None, "mp"),
            P(None, "mp", None),
            P(),
            P(None, "mp"),
            P(None, "mp"),
            P(None, None, "mp"),
            P(),
            P(),
            P("lat", None, "mp"),
        ),
        out_specs=(
            P("lat", None, "mp"),
            P("lat", None, "mp"),
            P("lat", None, "mp"),
            P("lat", "mp"),
            P("lat", "mp"),
            P("lat", "mp"),
        ),
        check_vma=False,
    )
```

time: 1300 us -> 586 us (0.45)
  waiting for transfers between devices: 878 us -> 41.6 us
  Pallas kernels: 0 us -> 271 us
  blocking collectives: 131 us -> 0 us
  local copies, waits for them, and re-layouts: 120 us -> 146 us
  matrix products: 79.3 us -> 59.6 us
  other arithmetic: 55.6 us -> 40.8 us
    psum x2 -> x0, waiting for transfers between devices: 333 us -> none  [group_sum(): return lax.psum(term.astype(jnp.bfloat16), 'mp').astype(jnp.float32)]
    reduce_scatter x6 -> x2, waiting for transfers between devices: 336 us -> 40.2 us  [shards(): lax.psum_scatter(part.astype(BF16), 'lat', scatter_dimension=0, tiled=True)]
    pallas_call x0 -> x7, Pallas kernels: none -> 271 us  [exchange(): pl.pallas_call(body, out_shape=[jax.ShapeDtypeStruct(shape, dtype) for sh...]
    all_gather x2, waiting for transfers between devices: 155 us -> 0.02 us  [the longest x1 0.02 us: shards(): expand_all = lax.all_gather(expand_weight, 'mp', axis=0)]
    psum x4 -> x0, blocking collectives: 131 us -> none  [feature_sums(): return lax.psum((first, second), 'mp')]
    ppermute x4 -> x0, waiting for transfers between devices: 54.5 us -> none  [passed_along(): return lax.ppermute(value, axis, pairs)]
    slice x5 -> x50, local copies, waits for them, and re-layouts: 9.77 us -> 36.8 us  [the longest x18 16.1 us: column_blocks(): ring[:, block * at:block * at + extent]]
    dot_general x19 -> x18, matrix products: 66.6 us -> 48 us  [the longest x1 4.48 us: shards(): jnp.einsum('wtd,mdce->wtmce', framed, qkv_all, preferred_element_type=F32)]
  transfers between devices with their start and end apart: 14 -> 4, of which waited for: 13 -> 1; matrix products, arithmetic and copies ran while one was open for 9% -> 31% of each run, Pallas kernels for 0% -> 27%
where the time goes in v1:
time: 586 us; the launch traced here: 575 us
  Pallas kernels  271 us (46%)
  local copies, waits for them, and re-layouts  146 us (25%)
  matrix products  59.6 us (10%)
  waiting for transfers between devices  41.6 us (7%)
  other arithmetic  40.8 us (7%)
  between operations  16.8 us (3%)
    pallas_call x7, Pallas kernels, exchange(): pl.pallas_call(body, out_shape=[jax.ShapeDtypeStruct(shape, dtype) for sh...  271 us
    reduce_scatter x2, waiting for transfers between devices, shards(): lax.psum_scatter(part.astype(BF16), 'lat', scatter_dimension=0, tiled=True)  40.2 us
    unnamed x154, local copies, waits for them, and re-layouts  31.9 us
    slice x18, local copies, waits for them, and re-layouts, column_blocks(): ring[:, block * at:block * at + extent]  16.1 us
  transfers between devices with their start and end apart: 4, of which 1 were waited for; matrix products, arithmetic and copies ran while one was open for 31% of the time, Pallas kernels for 27%

profile of v1, /device:TPU:1, one launch (start us, length us, event | category | flops | bytes accessed | tf_op | source)
XLA Modules:
  0.0 575.3 jit_solution(9839499894917817949)
XLA Ops:
  52.5 59.4 %shard_map.172 = (bf16[8,504,128]{2,1,0:T(8,128)(2,1)}, bf16[8,144,128]{2,1,0:T(8,128)(2,1)}, bf16[8,512,256]{2,1,0:T(8,128)(2,1)}, f32[8,8,128]{2,1,0:T(8,128)}) custom-call(bf16[8,504,128]{2,1,0:T(8,128)(2,1)} %maximum_maximum_fusion.refs_0_, bf16[8,144,128]{2,1,0:T(8,128)(2,1)} %pad_maximum_fusion.8.refs_1_, bf16[512,256]{1,0:T(8,128)(2,1)} %pad_maximum_fusion.9.refs_2_, ...), custom_call_target="tpu_custom_call" | custom-call | tf_op jit(solution)/shard_map/pallas_call | solution.py:67
  122.9 3.9 copy.299
  127.2 4.5 convolution_convert_fusion
  131.6 3.7 fusion.142
  155.7 16.7 %shard_map.173 = (bf16[216,512]{1,0:T(8,128)(2,1)}, bf16[144,512]{1,0:T(8,128)(2,1)}, bf16[72,512]{1,0:T(8,128)(2,1)}) custom-call(bf16[216,512]{1,0:T(8,128)(2,1)} %reshape.330.refs_0_, bf16[144,512]{1,0:T(8,128)(2,1)} %reshape.332.refs_1_, bf16[72,512]{1,0:T(8,128)(2,1)} %reshape.333.refs_2_), custom_call_target="tpu_custom_call" | custom-call | tf_op jit(solution)/shard_map/pallas_call | solution.py:67
  176.5 2.5 fusion.94
  183.9 2.7 multiply_reduce_fusion.4
  194.9 2.4 copy.293
  200.4 3.1 reshape_reshape.17
  203.5 3.3 copy.306
  214.3 8.5 %copy.366 = bf16[32,8,8,1024]{3,2,1,0:T(8,128)(2,1)} copy(bf16[32,8,8,1024]{3,1,2,0:T(8,128)(2,1)} %bitcast.259) | data formatting | bytes 8388608
  222.9 3.4 multiply_reduce_fusion.6
  229.0 50.1 %shard_map.174 = bf16[8,112,2048]{2,1,0:T(8,128)(2,1)} custom-call(bf16[112,2048]{1,0:T(8,128)(2,1)} %fusion.95.refs_0_), custom_call_target="tpu_custom_call" | custom-call | tf_op jit(solution)/shard_map/pallas_call | solution.py:67
  279.2 3.0 fusion.24
  283.5 2.4 fusion.38
  285.9 4.4 fusion.12
  295.2 42.8 %shard_map.175 = bf16[8,112,2048]{2,1,0:T(8,128)(2,1)} custom-call(bf16[8,112,2048]{2,1,0:T(8,128)(2,1)} %pad_maximum_fusion.refs_0_), custom_call_target="tpu_custom_call" | custom-call | tf_op jit(solution)/shard_map/pallas_call | solution.py:67
  338.0 2.9 convert_reduce_fusion
  344.8 2.6 copy.408
  349.7 2.8 copy.315
  360.9 20.7 %shard_map.176 = (bf16[216,512]{1,0:T(8,128)(2,1)}, bf16[144,512]{1,0:T(8,128)(2,1)}, bf16[72,512]{1,0:T(8,128)(2,1)}, bf16[8,216,128]{2,1,0:T(8,128)(2,1)}) custom-call(bf16[216,512]{1,0:T(8,128)(2,1)} %reshape.339.refs_0_, bf16[144,512]{1,0:T(8,128)(2,1)} %reshape.341.refs_1_, bf16[72,512]{1,0:T(8,128)(2,1)} %reshape.342.refs_2_, ...), custom_call_target="tpu_custom_call" | custom-call | tf_op jit(solution)/shard_map/pallas_call | solution.py:67
  386.4 2.6 convolution_convert_fusion.4
  391.8 4.1 fusion.55
  395.9 3.9 fusion.52
  399.8 2.4 fusion.59
  402.3 4.0 fusion.130
  415.0 3.8 bitcast_convert_fusion
  419.6 3.0 copy.335
  430.1 46.9 %shard_map.177 = (bf16[8,216,128]{2,1,0:T(8,128)(2,1)}, bf16[8,112,128]{2,1,0:T(8,128)(2,1)}, bf16[8,512,256]{2,1,0:T(8,128)(2,1)}) custom-call(bf16[8,216,128]{2,1,0:T(8,128)(2,1)} %pad_maximum_fusion.6.refs_0_, bf16[8,112,128]{2,1,0:T(8,128)(2,1)} %fusion.116.refs_1_, bf16[8,512,256]{2,1,0:T(8,128)(2,1)} %pad_maximum_fusion.2.refs_2_), custom_call_target="tpu_custom_call" | custom-call | tf_op jit(solution)/shard_map/pallas_call | solution.py:67
  482.5 2.7 reduce_sum.171
  485.2 33.9 %shard_map.178 = bf16[16,32,256]{2,1,0:T(8,128)(2,1)} custom-call(bf16[16,32,256]{2,1,0:T(8,128)(2,1)} %bitcast.294), custom_call_target="tpu_custom_call" | custom-call | tf_op jit(solution)/shard_map/pallas_call | solution.py:67
  526.7 40.2 %reduce-scatter.3.cloned.1.call-done = bf16[64,512]{1,0:T(8,128)(2,1)} async-done(((bf16[1024,512]{1,0:T(8,128)(2,1)}), bf16[64,512]{1,0:T(8,128)(2,1)}) %reduce-scatter.3.cloned.1.call-update) | async-done | bytes 65552 | tf_op jit(solution)/shard_map/reduce_scatter | solution.py:323
  (347 shorter events, 165.1 us)
Async XLA Ops:
  7.2 278.7 %copy-start = (bf16[1024,512]{1,0:T(8,128)(2,1)S(1)}, bf16[1024,512]{1,0:T(8,128)(2,1)}, u32[]{:S(2)}) copy-start(bf16[1024,512]{1,0:T(8,128)(2,1)} %param.21) | copy-start | bytes 3145732
  7.2 207.1 %all-gather.6.cloned.1.call-start = ((), (), s32[]{:S(2)}) async-start(), calls=%async_computation.5 | async-start | bytes 4718592 | tf_op jit(solution)/shard_map/all_gather | solution.py:212
  7.9 214.9 %all-gather.4.cloned.1.call-start = ((), (), s32[]{:S(2)}) async-start(), calls=%async_computation.2 | async-start | bytes 4718592 | tf_op jit(solution)/shard_map/all_gather | solution.py:211
  8.7 516.5 %reduce-scatter.5.cloned.1.call-start = ((), (), s32[]{:S(2)}) async-start(), calls=%async_computation.4 | async-start | bytes 1114112 | tf_op jit(solution)/shard_map/reduce_scatter | solution.py:323
  12.4 5.1 slice-start
  12.6 5.8 %copy-start.49 = (f32[4,64]{1,0:T(4,128)S(1)}, f32[4,64]{1,0:T(4,128)}, u32[]{:S(2)}) copy-start(f32[4,64]{1,0:T(4,128)} %param.17) | copy-start | bytes 3076
  12.6 5.8 %copy-start.51 = (f32[64]{0:T(128)S(1)}, f32[64]{0:T(128)}, u32[]{:S(2)}) copy-start(f32[64]{0:T(128)} %param.14) | copy-start | bytes 772
  15.9 8.6 %copy-start.21 = (bf16[12,36,64]{1,2,0:T(8,128)(2,1)S(1)}, bf16[12,36,64]{1,2,0:T(8,128)(2,1)}, u32[]{:S(2)}) copy-start(bf16[12,36,64]{1,2,0:T(8,128)(2,1)} %get-tuple-element.91) | copy-start | bytes 165892
  16.7 8.6 %copy-start.20 = (bf16[12,36,64]{1,2,0:T(8,128)(2,1)S(1)}, bf16[12,36,64]{1,2,0:T(8,128)(2,1)}, u32[]{:S(2)}) copy-start(bf16[12,36,64]{1,2,0:T(8,128)(2,1)} %get-tuple-element.90) | copy-start | bytes 165892
  22.6 12.0 %copy-start.27 = (bf16[12,48,64]{1,2,0:T(8,128)(2,1)S(1)}, bf16[12,48,64]{1,2,0:T(8,128)(2,1)}, u32[]{:S(2)}) copy-start(bf16[12,48,64]{1,2,0:T(8,128)(2,1)} %get-tuple-element.85) | copy-start | bytes 221188
  24.4 10.9 %copy-start.26 = (bf16[12,48,64]{1,2,0:T(8,128)(2,1)S(1)}, bf16[12,48,64]{1,2,0:T(8,128)(2,1)}, u32[]{:S(2)}) copy-start(bf16[12,48,64]{1,2,0:T(8,128)(2,1)} %get-tuple-element.84) | copy-start | bytes 221188
  24.6 11.5 %copy-start.25 = (bf16[12,48,64]{1,2,0:T(8,128)(2,1)S(1)}, bf16[12,48,64]{1,2,0:T(8,128)(2,1)}, u32[]{:S(2)}) copy-start(bf16[12,48,64]{1,2,0:T(8,128)(2,1)} %get-tuple-element.83) | copy-start | bytes 221188
  25.3 11.6 %copy-start.24 = (bf16[12,48,64]{1,2,0:T(8,128)(2,1)S(1)}, bf16[12,48,64]{1,2,0:T(8,128)(2,1)}, u32[]{:S(2)}) copy-start(bf16[12,48,64]{1,2,0:T(8,128)(2,1)} %get-tuple-element.82) | copy-start | bytes 221188
  26.1 11.6 %copy-start.22 = (bf16[12,48,64]{1,2,0:T(8,128)(2,1)S(1)}, bf16[12,48,64]{1,2,0:T(8,128)(2,1)}, u32[]{:S(2)}) copy-start(bf16[12,48,64]{1,2,0:T(8,128)(2,1)} %get-tuple-element.71) | copy-start | bytes 221188
  39.4 9.5 %copy-start.30 = (bf16[12,48,64]{2,1,0:T(8,128)(2,1)S(1)}, bf16[12,48,64]{2,1,0:T(8,128)(2,1)}, u32[]{:S(2)}) copy-start(bf16[12,48,64]{2,1,0:T(8,128)(2,1)} %copy.277) | copy-start | bytes 221188
  39.4 9.6 %copy-start.28 = (bf16[12,48,64]{2,1,0:T(8,128)(2,1)S(1)}, bf16[12,48,64]{2,1,0:T(8,128)(2,1)}, u32[]{:S(2)}) copy-start(bf16[12,48,64]{2,1,0:T(8,128)(2,1)} %copy.278) | copy-start | bytes 221188
  40.6 8.5 %copy-start.29 = (bf16[12,48,64]{2,1,0:T(8,128)(2,1)S(1)}, bf16[12,48,64]{2,1,0:T(8,128)(2,1)}, u32[]{:S(2)}) copy-start(bf16[12,48,64]{2,1,0:T(8,128)(2,1)} %copy.279) | copy-start | bytes 221188
  41.3 7.5 %copy-start.33 = (bf16[12,48,64]{2,1,0:T(8,128)(2,1)S(1)}, bf16[12,48,64]{2,1,0:T(8,128)(2,1)}, u32[]{:S(2)}) copy-start(bf16[12,48,64]{2,1,0:T(8,128)(2,1)} %copy.274) | copy-start | bytes 221188
  41.3 7.5 %copy-start.32 = (bf16[12,48,64]{2,1,0:T(8,128)(2,1)S(1)}, bf16[12,48,64]{2,1,0:T(8,128)(2,1)}, u32[]{:S(2)}) copy-start(bf16[12,48,64]{2,1,0:T(8,128)(2,1)} %copy.275) | copy-start | bytes 221188
  41.3 7.6 %copy-start.31 = (bf16[12,48,64]{2,1,0:T(8,128)(2,1)S(1)}, bf16[12,48,64]{2,1,0:T(8,128)(2,1)}, u32[]{:S(2)}) copy-start(bf16[12,48,64]{2,1,0:T(8,128)(2,1)} %copy.276) | copy-start | bytes 221188
  42.3 6.8 %copy-start.34 = (bf16[512,64]{1,0:T(8,128)(2,1)S(1)}, bf16[512,64]{1,0:T(8,128)(2,1)}, u32[]{:S(2)}) copy-start(bf16[512,64]{1,0:T(8,128)(2,1)} %copy.291) | copy-start | bytes 196612
  122.9 4.2 copy-start.39
  147.5 29.0 %copy-start.12 = (bf16[12,36,512]{2,1,0:T(8,128)(2,1)S(1)}, bf16[12,36,512]{2,1,0:T(8,128)(2,1)}, u32[]{:S(2)}) copy-start(bf16[12,36,512]{2,1,0:T(8,128)(2,1)} %reshape.331) | copy-start | bytes 1327108
  180.8 13.1 %copy-start.18 = (bf16[8,216,128]{2,1,0:T(8,128)(2,1)S(1)}, bf16[8,216,128]{2,1,0:T(8,128)(2,1)}, u32[]{:S(2)}) copy-start(bf16[8,216,128]{2,1,0:T(8,128)(2,1)} %slice.216) | copy-start | bytes 1327108
  214.3 8.6 %copy-start.40 = (f32[4,512]{1,0:T(4,128)S(1)}, f32[4,512]{1,0:T(4,128)}, u32[]{:S(2)}) copy-start(f32[4,512]{1,0:T(4,128)} %mul.244) | copy-start | bytes 24580
  279.1 4.3 copy-start.8
  285.9 4.4 copy-start.58
  359.1 25.4 %copy-start.14 = (bf16[12,36,512]{2,1,0:T(8,128)(2,1)S(1)}, bf16[12,36,512]{2,1,0:T(8,128)(2,1)}, u32[]{:S(2)}) copy-start(bf16[12,36,512]{2,1,0:T(8,128)(2,1)} %copy-done.13) | copy-start | bytes 1327108
  386.4 5.4 copy-start.37
  402.2 164.6 %reduce-scatter.3.cloned.1.call-start = ((), (), s32[]{:S(2)}) async-start(), calls=%async_computation.3 | async-start | bytes 1114112 | tf_op jit(solution)/shard_map/reduce_scatter | solution.py:323
  482.5 39.0 %copy-start.17 = (bf16[8,216,128]{2,1,0:T(8,128)(2,1)S(1)}, bf16[8,216,128]{2,1,0:T(8,128)(2,1)}, u32[]{:S(2)}) copy-start(bf16[8,216,128]{2,1,0:T(8,128)(2,1)} %get-tuple-element.27) | copy-start | bytes 1327108
  522.1 46.2 %copy-start.1 = (bf16[1024,512]{1,0:T(8,128)(2,1)S(1)}, bf16[1024,512]{1,0:T(8,128)(2,1)}, u32[]{:S(2)}) copy-start(bf16[1024,512]{1,0:T(8,128)(2,1)} %param.21) | copy-start | bytes 3145732
  (37 other events, 85.0 us)
Sparse Core Ops, SparseCore 0:
  10.4 111.5 all-gather.5
  124.3 76.0 all-gather.3
  402.3 106.1 reduce-scatter.4
  510.9 55.8 reduce-scatter.2

commit v2 on v1

v2 whole, which is shorter than its diff:
```python
import jax
import jax.numpy as jnp
from jax import lax
from jax.experimental import pallas as pl
from jax.experimental.pallas import tpu as pltpu
from jax.sharding import PartitionSpec as P

WIN_H = 6
WIN_W = 12
HDIM = 64
EPSILON = 1e-05
MASKED = -1e30
BF16 = jnp.bfloat16
F32 = jnp.float32


def exchange(collective, inputs, outputs, moves):
    n_lat, n_mp = lax.axis_size("lat"), lax.axis_size("mp")
    steps = []
    for move in moves:
        if move[4:] != (0, 0) and move[4:] not in steps:
            steps.append(move[4:])

    def part_of(ref, part, place):
        if part is None:
            return ref
        if part == "core":
            half = ref.shape[2] // 2
            return ref.at[:, :, pl.ds(pl.multiple_of(place["core"] * half, half), half)]
        if isinstance(part, str):
            return ref.at[place[part]]
        if isinstance(part[0], str):
            axis, size = part
            return ref.at[:, pl.ds(pl.multiple_of(place[axis] * size, size), size)]
        return ref.at[part]

    def body(*refs):
        sources = refs[: len(inputs)]
        landings = refs[len(inputs) : len(inputs) + len(outputs)]
        send, receive = refs[-2:]
        lat, mp = lax.axis_index("lat"), lax.axis_index("mp")
        here = {"lat": lat, "mp": mp, "core": lax.rem(lat, 2)}

        def reached(down, right):
            if down == "sibling":
                return {"lat": lat + 1 - 2 * here["core"], "mp": mp}
            return {
                "lat": lax.rem(lat + n_lat + down, n_lat),
                "mp": lax.rem(mp + n_mp + right, n_mp),
            }

        barrier = pltpu.get_barrier_semaphore()
        for down, right in steps:
            source = reached(down if down == "sibling" else -down, -right)
            pl.semaphore_signal(
                barrier,
                inc=1,
                device_id=(source["lat"], source["mp"]),
                device_id_type=pl.DeviceIdType.MESH,
            )
        pl.semaphore_wait(barrier, len(steps))
        copies = []
        for index, (source, source_part, landing, landing_part, down, right) in enumerate(moves):
            target = reached(down, right)
            source_ref = part_of(sources[source], source_part, target)
            landing_ref = part_of(landings[landing], landing_part, here)
            if (down, right) == (0, 0):
                copy = pltpu.make_async_copy(source_ref, landing_ref, receive.at[index])
            else:
                copy = pltpu.make_async_remote_copy(
                    src_ref=source_ref,
                    dst_ref=landing_ref,
                    send_sem=send.at[index],
                    recv_sem=receive.at[index],
                    device_id=(target["lat"], target["mp"]),
                    device_id_type=pl.DeviceIdType.MESH,
                )
            copy.start()
            copies.append(copy)
        for copy in copies:
            copy.wait()

    return pl.pallas_call(
        body,
        out_shape=[jax.ShapeDtypeStruct(shape, dtype) for shape, dtype in outputs],
        in_specs=[pl.BlockSpec(memory_space=pl.ANY)] * len(inputs),
        out_specs=[pl.BlockSpec(memory_space=pl.ANY)] * len(outputs),
        scratch_shapes=[
            pltpu.SemaphoreType.DMA((len(moves),)),
            pltpu.SemaphoreType.DMA((len(moves),)),
        ],
        compiler_params=pltpu.CompilerParams(collective_id=collective, has_side_effects=True),
    )(*inputs)


def local_kernel(body, operands, outputs, scratch=(), scalars=0):
    spaces = [pltpu.SMEM] * scalars + [pltpu.VMEM] * (len(operands) - scalars)
    return pl.pallas_call(
        body,
        out_shape=[jax.ShapeDtypeStruct(shape, dtype) for shape, dtype in outputs],
        in_specs=[pl.BlockSpec(memory_space=space) for space in spaces],
        out_specs=[pl.BlockSpec(memory_space=pltpu.VMEM)] * len(outputs),
        scratch_shapes=list(scratch),
        compiler_params=pltpu.CompilerParams(vmem_limit_bytes=48 * 1024 * 1024),
    )(*operands)


def dot_nn(left, right):
    return lax.dot_general(left, right, (((1,), (0,)), ((), ())), preferred_element_type=F32)


def dot_nt(left, right):
    return lax.dot_general(left, right, (((1,), (1,)), ((), ())), preferred_element_type=F32)


def dot_tn(left, right):
    return lax.dot_general(left, right, (((0,), (0,)), ((), ())), preferred_element_type=F32)


def halves_beside(values):
    half = values.shape[-2] // 2
    return jnp.concatenate([values[..., :half, :], values[..., half:, :]], axis=-1)


def groups_joined(slabs):
    count, half, _ = slabs.shape
    view = slabs.reshape(count, half, 2, HDIM).transpose(2, 1, 0, 3)
    return view.reshape(2 * half, count * HDIM)


def to_windows(grid):
    row_count, lon_count = (grid.shape[0], grid.shape[1])
    trailing = grid.shape[2:]
    view = grid.reshape((row_count // WIN_H, WIN_H, lon_count // WIN_W, WIN_W) + trailing)
    view = jnp.swapaxes(view, 1, 2)
    return view.reshape(((row_count // WIN_H) * (lon_count // WIN_W), WIN_H * WIN_W) + trailing)


def from_windows(windows):
    bands, columns, _, width = windows.shape
    view = windows.reshape((bands, columns, WIN_H, WIN_W, width))
    view = jnp.swapaxes(view, 1, 2)
    return view.reshape((bands * WIN_H, columns * WIN_W, width))


def merge_patches(grid, padded):
    row_count, lon_count, features = grid.shape
    view = grid.reshape(row_count // 2, 2, lon_count // 2, 2, features)
    view = view.transpose(1, 3, 0, 2, 4).reshape(4, row_count * lon_count // 4, features)
    return jnp.pad(view, ((0, 0), (0, padded - view.shape[1]), (0, 0)))


def norm_stats(values, count):
    center = sum(jnp.sum(value, axis=1, keepdims=True) for value in values) / count
    second = sum(jnp.sum(value * value, axis=1, keepdims=True) for value in values) / count
    return (center, lax.rsqrt(second - center * center + EPSILON))


def norm_backward(grads, gains, units, scale_inv, count):
    scaled = [grad * gain for grad, gain in zip(grads, gains)]
    first = sum(jnp.sum(value, axis=1, keepdims=True) for value in scaled) / count
    second = (
        sum(jnp.sum(value * unit, axis=1, keepdims=True) for value, unit in zip(scaled, units))
        / count
    )
    return [scale_inv * (value - first - unit * second) for value, unit in zip(scaled, units)]


def pair_slabs(upper, lower, out_ref, first_rows):
    low = lax.broadcasted_iota(jnp.int32, (upper.shape[0], 2 * HDIM), 1) < HDIM
    rows = pl.ds(first_rows, upper.shape[0])
    for pair in range(upper.shape[1] // (2 * HDIM)):
        lanes = slice(2 * HDIM * pair, 2 * HDIM * (pair + 1))
        one, two = upper[:, lanes], lower[:, lanes]
        swapped_one = jnp.concatenate([one[:, HDIM:], one[:, :HDIM]], axis=1)
        swapped_two = jnp.concatenate([two[:, HDIM:], two[:, :HDIM]], axis=1)
        out_ref[2 * pair, rows, :] = jnp.where(low, one, swapped_two).astype(BF16)
        out_ref[2 * pair + 1, rows, :] = jnp.where(low, swapped_one, two).astype(BF16)


WIN = WIN_H * WIN_W
FACTOR = HDIM ** (-0.5)


def heads_apart(values):
    low = lax.broadcasted_iota(jnp.int32, values.shape, 1) < HDIM
    zero = jnp.zeros_like(values)
    both = [jnp.where(low, values, zero), jnp.where(low, zero, values)]
    return jnp.concatenate(both, axis=0).astype(BF16)


def heads_together(values):
    low = lax.broadcasted_iota(jnp.int32, (WIN, 2 * HDIM), 1) < HDIM
    return jnp.where(low, values[:WIN], values[WIN:])


def window_probs(cut, window, query, keys):
    scores = dot_nt(query, keys) * FACTOR
    spot = lax.broadcasted_iota(jnp.int32, scores.shape, 0)
    spot = jnp.where(spot >= WIN, spot - WIN, spot)
    other = lax.broadcasted_iota(jnp.int32, scores.shape, 1)
    edge = cut * WIN_W - jnp.where(window >= 3, WIN, 0)
    same = (spot >= edge) == (other >= edge)
    scores = jnp.where(same, scores, MASKED)
    weights = jnp.exp(scores - jnp.max(scores, axis=1, keepdims=True))
    return weights / jnp.sum(weights, axis=1, keepdims=True)


def framed_packed(fields_ref, gain_ref, weights_ref, packed):
    values = fields_ref[...].astype(F32)
    center, scale_inv = norm_stats([values], values.shape[1])
    unit = (values - center) * scale_inv
    framed = (unit * gain_ref[...]).astype(BF16)
    for kind in range(3):
        packed[kind] = dot_nt(framed, weights_ref[kind]).astype(BF16).astype(F32)
    return (framed, unit, scale_inv)


def window_parts(refs, window, pair):
    rows = pl.ds(pl.multiple_of(window * WIN, 8), WIN)
    lanes = slice(2 * HDIM * pair, 2 * HDIM * (pair + 1))
    return [ref[rows, lanes] for ref in refs]


def attention_forward(cut_ref, fields_ref, gain_ref, weights_ref, out_ref, context_ref, packed, held):
    framed_packed(fields_ref, gain_ref, weights_ref, packed)
    cut = cut_ref[0]
    windows = fields_ref.shape[0] // WIN

    def step(window, carry):
        rows = pl.ds(pl.multiple_of(window * WIN, 8), WIN)
        for pair in range(fields_ref.shape[1] // (2 * HDIM)):
            query, keys, values = window_parts([packed.at[kind] for kind in range(3)], window, pair)
            probs = window_probs(cut, window, heads_apart(query), keys.astype(BF16))
            joined = dot_nn(probs.astype(BF16), values.astype(BF16))
            held[rows, 2 * HDIM * pair : 2 * HDIM * (pair + 1)] = heads_together(joined)
        return carry

    lax.fori_loop(0, windows, step, 0)
    context = held[...].astype(BF16)
    context_ref[...] = context
    out_ref[...] = dot_nn(context, weights_ref[3]).astype(BF16)


def attention_backward(
    cut_ref, fields_ref, gain_ref, weights_ref, context_ref, grad_ref, slab_ref, weight_ref,
    packed, grads, held,
):
    framed, unit, scale_inv = framed_packed(fields_ref, gain_ref, weights_ref, packed)
    cut = cut_ref[0]
    windows = fields_ref.shape[0] // WIN
    grad_framed = grad_ref[...]
    held[...] = dot_nt(grad_framed, weights_ref[3]).astype(BF16).astype(F32)

    def step(window, carry):
        rows = pl.ds(pl.multiple_of(window * WIN, 8), WIN)
        for pair in range(fields_ref.shape[1] // (2 * HDIM)):
            lanes = slice(2 * HDIM * pair, 2 * HDIM * (pair + 1))
            query, keys, values, grad = window_parts(
                [packed.at[kind] for kind in range(3)] + [held], window, pair
            )
            query, grad = heads_apart(query), heads_apart(grad)
            keys, values = keys.astype(BF16), values.astype(BF16)
            probs = window_probs(cut, window, query, keys)
            grad_probs = dot_nt(grad, values)
            inner = jnp.sum(grad_probs * probs, axis=1, keepdims=True)
            grad_scores = (probs * (grad_probs - inner) * FACTOR).astype(BF16)
            grads[0, rows, lanes] = heads_together(dot_nn(grad_scores, keys))
            grads[1, rows, lanes] = dot_tn(grad_scores, query)
            grads[2, rows, lanes] = dot_tn(probs.astype(BF16), grad)
        return carry

    lax.fori_loop(0, windows, step, 0)
    grad_normed = jnp.zeros(fields_ref.shape, F32)
    for kind in range(3):
        grad_kind = grads[kind].astype(BF16)
        weight_ref[kind] = dot_tn(grad_kind, framed).astype(BF16)
        grad_normed = grad_normed + dot_nn(grad_kind, weights_ref[kind])
    weight_ref[3] = dot_tn(context_ref[...], grad_framed).astype(BF16)
    (back,) = norm_backward([grad_normed], [gain_ref[...]], [unit], scale_inv, unit.shape[1])
    result = grad_framed.astype(F32) + back
    half = result.shape[0] // 2
    pair_slabs(result[:half], result[half:], slab_ref, 0)


def merge_forward(
    fields_ref, attention_ref, cot_ref, gain_ref, mlp_gain_ref, weights_ref,
    pair_ref, hidden_ref, merged_ref, grad_ref,
):
    width_two = merged_ref.shape[1]
    hidden = []
    for patch in range(4):
        value = fields_ref[patch].astype(F32) + attention_ref[patch].astype(F32)
        hidden_ref[patch] = value.astype(BF16)
        hidden.append(value.astype(BF16).astype(F32))
    center, scale_inv = norm_stats(hidden, 4 * hidden[0].shape[1])
    merged = jnp.zeros(merged_ref.shape, F32)
    grad = jnp.zeros(merged_ref.shape, F32)
    for patch in range(4):
        normed = (hidden[patch] - center) * scale_inv * gain_ref[patch : patch + 1, :]
        merged = merged + dot_nn(normed.astype(BF16), weights_ref[patch])
        grad = grad + dot_nn(cot_ref[patch], weights_ref[4 + patch])
    merged_ref[...] = merged.astype(BF16)
    merged = merged.astype(BF16).astype(F32)
    center, scale_inv = norm_stats([merged], width_two)
    mlp_in = (merged - center) * scale_inv * mlp_gain_ref[...]
    pair_ref[:, :width_two] = mlp_in.astype(BF16)
    pair_ref[:, width_two:] = grad.astype(BF16)
    grad_ref[...] = grad


def merge_backward(
    parts_ref, merged_ref, grad_ref, hidden_ref, cot_ref, gain_ref, mlp_gain_ref, weights_ref,
    slab_ref, out_ref,
):
    width_two = merged_ref.shape[1]
    count = merged_ref.shape[0]
    total = parts_ref[0].astype(F32)
    for index in range(1, parts_ref.shape[0]):
        total = total + parts_ref[index].astype(F32)
    merged = merged_ref[...].astype(F32)
    bottom = (merged + total[:, :width_two]).astype(BF16)
    decoded = [
        hidden_ref[patch].astype(F32) + dot_nt(bottom, weights_ref[4 + patch])
        for patch in range(4)
    ]
    for side in range(2):
        pair_slabs(decoded[side], decoded[2 + side], slab_ref, side * count)
    center, scale_inv = norm_stats([merged], width_two)
    unit = (merged - center) * scale_inv
    (back,) = norm_backward(
        [total[:, width_two:]], [mlp_gain_ref[...]], [unit], scale_inv, width_two
    )
    grad_merged = (grad_ref[...] + back).astype(BF16)
    hidden = [hidden_ref[patch].astype(F32) for patch in range(4)]
    center, scale_inv = norm_stats(hidden, 4 * hidden[0].shape[1])
    units = [(value - center) * scale_inv for value in hidden]
    backs = norm_backward(
        [dot_nt(grad_merged, weights_ref[patch]) for patch in range(4)],
        [gain_ref[patch : patch + 1, :] for patch in range(4)],
        units,
        scale_inv,
        4 * hidden[0].shape[1],
    )
    for patch in range(4):
        out_ref[patch] = (cot_ref[patch].astype(F32) + backs[patch]).astype(BF16)


def shards(
    fields,
    first_gain,
    qkv_weight,
    proj_weight,
    merge_gain,
    merge_weight,
    mlp_gain,
    up_weight,
    down_weight,
    expand_weight,
    lat_shift,
    lon_shift,
    cotangent,
):
    n_lat, n_mp = lax.axis_size("lat"), lax.axis_size("mp")
    lat, core = lax.axis_index("lat"), lax.rem(lax.axis_index("lat"), 2)
    lat_offset = lat_shift[0]
    lon_offset = lon_shift[0]
    rows, lon_count, group = fields.shape
    width = group * n_mp
    block = lon_count // n_mp
    wide = block + WIN_W
    bands, columns = rows // WIN_H, block // WIN_W
    tokens = rows * block
    width_two = merge_weight.shape[2]
    span = up_weight.shape[1]
    merged_count = tokens // 4
    padded = -(-merged_count // 16) * 16
    others = range(n_mp)

    section = jnp.concatenate([merge_weight, expand_weight.transpose(1, 2, 0)], axis=0)
    half_section = lax.dynamic_slice_in_dim(section, core * (group // 2), group // 2, 1)
    half_all = lax.all_gather(half_section, "mp", axis=1)

    blocks = fields.reshape(rows, n_mp, block, group).transpose(1, 0, 2, 3)
    margin = jnp.roll(blocks[:, :, :WIN_W], -1, axis=0)
    field_blocks = jnp.concatenate([blocks, margin], axis=2)
    body_slab = halves_beside(field_blocks.reshape(n_mp, rows * wide, group))
    edge_slab = halves_beside(field_blocks[:, :WIN_H].reshape(n_mp, WIN_H * wide, group))
    cot_blocks = cotangent.reshape(rows, n_mp, block, group).transpose(1, 0, 2, 3)
    cot_slab = halves_beside(cot_blocks.reshape(n_mp, tokens, group))
    weights = jnp.concatenate(
        [qkv_weight.transpose(1, 2, 0), proj_weight.transpose(1, 0)[None]], axis=0
    )
    gains = jnp.pad(jnp.concatenate([first_gain[None], merge_gain], axis=0), ((0, 3), (0, 64)))
    body_got, edge_got, cot_got, weights_all, gains_all = exchange(
        1,
        [body_slab, edge_slab, cot_slab, weights, gains],
        [
            (body_slab.shape, BF16),
            (edge_slab.shape, BF16),
            (cot_slab.shape, BF16),
            ((4, width, width), BF16),
            ((n_mp,) + gains.shape, F32),
        ],
        [(4, None, 4, "mp", 0, step) for step in others]
        + [(0, "mp", 0, "mp", 0, step) for step in others]
        + [(1, "mp", 1, "mp", -1, step) for step in others]
        + [(3, None, 3, ("mp", group), 0, step) for step in others]
        + [(2, "mp", 2, "mp", 0, step) for step in others],
    )
    body = groups_joined(body_got).reshape(rows, wide, width)
    edge = groups_joined(edge_got).reshape(WIN_H, wide, width)
    cot = groups_joined(cot_got).reshape(rows, block, width)
    first_all = gains_all[:, 0, :group].reshape(1, width)
    merge_gain_all = gains_all[:, 1:5, :group].transpose(1, 0, 2).reshape(4, width)
    mlp_gain_row = mlp_gain.reshape(1, width_two)
    own_fields = merge_patches(body[:, :block], padded)
    cot_patches = merge_patches(cot, padded)

    def into_frame(whole):
        part = lax.dynamic_slice(
            whole, (lat_offset, lon_offset, jnp.int32(0)), (rows, block, width)
        )
        return to_windows(part).reshape(tokens, width)

    framed_fields = into_frame(jnp.concatenate([body, edge], axis=0))
    cut = (jnp.int32(rows) * (n_lat - lat) - lat_offset).reshape(1)
    attention_framed, context = local_kernel(
        attention_forward,
        [cut, framed_fields, first_all, weights_all],
        [((tokens, width), BF16), ((tokens, width), BF16)],
        [pltpu.VMEM((3, tokens, width), F32), pltpu.VMEM((tokens, width), F32)],
        scalars=1,
    )
    window_shape = (bands, columns, WIN, width)
    around = (bands + 1, columns + 1, WIN, width)
    halo, section_all = exchange(
        2,
        [attention_framed.reshape(window_shape), half_all],
        [(around, BF16), ((8, n_mp, group, width_two), BF16)],
        [
            (0, (bands - 1, columns - 1), 0, (0, 0), 1, 1),
            (0, (slice(0, bands), columns - 1), 0, (slice(1, bands + 1), 0), 0, 1),
            (0, (bands - 1,), 0, (0, slice(1, columns + 1)), 1, 0),
            (1, None, 1, "core", "sibling", 0),
            (1, None, 1, "core", 0, 0),
            (0, None, 0, (slice(1, bands + 1), slice(1, columns + 1)), 0, 0),
        ],
    )
    section_all = section_all.reshape(8, width, width_two)
    attention = lax.dynamic_slice(
        from_windows(halo),
        (WIN_H - lat_offset, WIN_W - lon_offset, jnp.int32(0)),
        (rows, block, width),
    )
    pair, hidden, merged, grad_bottom = local_kernel(
        merge_forward,
        [
            own_fields,
            merge_patches(attention, padded),
            cot_patches,
            merge_gain_all,
            mlp_gain_row,
            section_all,
        ],
        [
            ((padded, 2 * width_two), BF16),
            ((4, padded, width), BF16),
            ((padded, width_two), BF16),
            ((padded, width_two), F32),
        ],
    )
    (pairs,) = exchange(
        3,
        [pair],
        [((n_mp,) + pair.shape, BF16)],
        [(0, None, 0, "mp", 0, step) for step in others],
    )
    pairs = pairs.reshape(n_mp * padded, 2 * width_two)
    mlp_in, bottom_grad = pairs[:, :width_two], pairs[:, width_two:]
    hidden_up = jnp.dot(mlp_in, up_weight, preferred_element_type=F32)
    activated = jax.nn.gelu(hidden_up).astype(BF16)
    grad_act = jnp.dot(bottom_grad, down_weight, preferred_element_type=F32)
    gelu_back = jax.vjp(jax.nn.gelu, hidden_up)[1]
    grad_pre = gelu_back(grad_act)[0].astype(BF16)
    terms = jnp.concatenate(
        [
            jnp.einsum("af,ef->ae", activated, down_weight, preferred_element_type=F32),
            jnp.einsum("af,ef->ae", grad_pre, up_weight, preferred_element_type=F32),
        ],
        axis=1,
    ).astype(BF16)
    (parts,) = exchange(
        4,
        [terms.reshape(n_mp, padded, 2 * width_two)],
        [((n_mp, padded, 2 * width_two), BF16)],
        [(0, "mp", 0, "mp", 0, step) for step in others],
    )
    down_local = jnp.einsum("ao,af->of", bottom_grad, activated, preferred_element_type=F32)
    up_local = jnp.einsum("ae,af->ef", mlp_in, grad_pre, preferred_element_type=F32)
    decoded_slab, grad_hidden = local_kernel(
        merge_backward,
        [
            parts,
            merged,
            grad_bottom,
            hidden,
            cot_patches,
            merge_gain_all,
            mlp_gain_row,
            section_all,
        ],
        [((n_mp, 2 * padded, 2 * group), BF16), ((4, padded, width), BF16)],
    )
    grad_windows = grad_hidden[:, :merged_count].reshape(
        2, 2, bands, WIN_H // 2, columns, WIN_W // 2, width
    )
    grad_windows = grad_windows.transpose(2, 4, 3, 0, 5, 1, 6).reshape(window_shape)
    halo, decoded_got = exchange(
        5,
        [grad_windows, decoded_slab],
        [(around, BF16), (decoded_slab.shape, BF16)],
        [
            (0, (0, 0), 0, (bands, columns), -1, -1),
            (0, (slice(0, bands), 0), 0, (slice(0, bands), columns), 0, -1),
            (0, (0,), 0, (bands, slice(0, columns)), -1, 0),
            (0, None, 0, (slice(0, bands), slice(0, columns)), 0, 0),
        ]
        + [(1, "mp", 1, "mp", 0, step) for step in others],
    )
    grad_framed = into_frame(from_windows(halo))
    grad_slab, weight_grads = local_kernel(
        attention_backward,
        [cut, framed_fields, first_all, weights_all, context, grad_framed],
        [((n_mp, tokens // 2, 2 * group), BF16), ((4, width, width), BF16)],
        [
            pltpu.VMEM((3, tokens, width), F32),
            pltpu.VMEM((3, tokens, width), F32),
            pltpu.VMEM((tokens, width), F32),
        ],
        scalars=1,
    )
    large = (n_lat, width_two // n_lat, span)
    grad_got, edge_got, weight_got, up_got, down_got = exchange(
        6,
        [
            grad_slab,
            weight_grads,
            up_local.astype(BF16).reshape(large),
            down_local.astype(BF16).reshape(large),
        ],
        [
            (grad_slab.shape, BF16),
            (grad_slab.shape, BF16),
            ((n_mp, 4, group, width), BF16),
            (large, BF16),
            (large, BF16),
        ],
        [(1, ("mp", group), 2, "mp", 0, step) for step in others]
        + [(2, "lat", 3, "lat", step, 0) for step in range(n_lat)]
        + [(3, "lat", 4, "lat", step, 0) for step in range(n_lat)]
        + [(0, "mp", 0, "mp", 0, step) for step in others]
        + [(0, "mp", 1, "mp", 1, step) for step in others],
    )
    weight_sum = jnp.sum(weight_got.astype(F32), axis=0).astype(BF16)
    weight_sum = weight_sum.reshape(4 * group, width).transpose(1, 0)
    (lat_got,) = exchange(
        7,
        [weight_sum.reshape(n_lat, width // n_lat, 4 * group)],
        [((n_lat, width // n_lat, 4 * group), BF16)],
        [(0, "lat", 0, "lat", step, 0) for step in range(n_lat)],
    )
    grad_up = jnp.sum(up_got.astype(F32), axis=0)
    grad_down = jnp.sum(down_got.astype(F32), axis=0)
    weight_total = jnp.sum(lat_got.astype(F32), axis=0)
    grad_qkv = weight_total[:, : 3 * group].reshape(width // n_lat, 3, group)
    grad_proj = weight_total[:, 3 * group :]
    decoded_view = decoded_got.reshape(n_mp, 2, padded, 2, group)[:, :, :merged_count]
    decoded_view = decoded_view.reshape(n_mp, 2, rows // 2, block // 2, 2, group)
    decoded = decoded_view.transpose(2, 4, 0, 3, 1, 5).reshape(rows, lon_count, group)

    def columns_joined(slabs):
        view = slabs.reshape(n_mp, columns, WIN_H, WIN_W, -1, group)
        return view.transpose(4, 2, 0, 1, 3, 5).reshape(-1, lon_count, group)

    grad_rows = jnp.concatenate(
        [columns_joined(edge_got[..., group:]), columns_joined(grad_got)], axis=0
    )
    grad_rows = jnp.concatenate([grad_rows[:, -WIN_W:], grad_rows], axis=1)
    grad_input = lax.dynamic_slice(
        grad_rows,
        (WIN_H - lat_offset, WIN_W - lon_offset, jnp.int32(0)),
        (rows, lon_count, group),
    ).astype(F32)
    return (decoded, grad_input, grad_qkv, grad_proj, grad_up, grad_down)


def solution(mesh):
    return jax.shard_map(
        shards,
        mesh=mesh,
        in_specs=(
            P("lat", None, "mp"),
            P("mp"),
            P(None, None, "mp"),
            P(None, "mp"),
            P(None, "mp"),
            P(None, "mp", None),
            P(),
            P(None, "mp"),
            P(None, "mp"),
            P(None, None, "mp"),
            P(),
            P(),
            P("lat", None, "mp"),
        ),
        out_specs=(
            P("lat", None, "mp"),
            P("lat", None, "mp"),
            P("lat", None, "mp"),
            P("lat", "mp"),
            P("lat", "mp"),
            P("lat", "mp"),
        ),
        check_vma=False,
    )
```

time: 586 us -> 600 us (1.024)
  Pallas kernels: 271 us -> 456 us
  local copies, waits for them, and re-layouts: 146 us -> 80 us
  matrix products: 59.6 us -> 12.1 us
  waiting for transfers between devices: 41.6 us -> 11.6 us
  other arithmetic: 40.8 us -> 14.7 us
    pallas_call x7, Pallas kernels: 271 us -> 422 us  [exchange(): pl.pallas_call(body, out_shape=[jax.ShapeDtypeStruct(shape, dtype) for sh...]
    reduce_scatter x2 -> x0, waiting for transfers between devices: 40.2 us -> none  [shards(): lax.psum_scatter(part.astype(BF16), 'lat', scatter_dimension=0, tiled=True)]
    dot_general x14 -> x0, matrix products: 39.2 us -> none  [the longest x1 4.48 us: shards(): jnp.einsum('wtd,mdce->wtmce', framed, qkv_all, preferred_element_type=F32)]
    pallas_call x0 -> x4, Pallas kernels: none -> 33.8 us  [local_kernel(): pl.pallas_call(body, out_shape=[jax.ShapeDtypeStruct(shape, dtype) for sh...]
    slice x40 -> x7, local copies, waits for them, and re-layouts: 32.6 us -> 4.38 us  [the longest x1 1.83 us: shards(): decoded_got.reshape(n_mp, 2, padded, 2, group)[:, :, :merged_count]]
    convert_element_type x11 -> x0, local copies, waits for them, and re-layouts: 14.4 us -> none  [the longest x3 4.86 us: shards(): hidden_wide = hidden.astype(F32)]
    another operation x19 -> x5, local copies, waits for them, and re-layouts: 17.2 us -> 3.14 us  [the longest x2 2.03 us: into_frame(): return to_windows(part).reshape(tokens, width)]
    all_gather x2 -> x1, waiting for transfers between devices: 0.02 us -> 11.5 us  [shards(): half_all = lax.all_gather(half_section, 'mp', axis=1)]
  transfers between devices with their start and end apart: 4 -> 1, of which waited for: 1 -> 1; matrix products, arithmetic and copies ran while one was open for 31% -> 5% of each run, Pallas kernels for 27% -> 11%
where the time goes in v2:
time: 600 us; the launch traced here: 590 us
  Pallas kernels  456 us (76%)
  local copies, waits for them, and re-layouts  80 us (13%)
  between operations  16.4 us (3%)
  other arithmetic  14.7 us (2%)
  matrix products  12.1 us (2%)
  waiting for transfers between devices  11.6 us (2%)
    pallas_call x7, Pallas kernels, exchange(): pl.pallas_call(body, out_shape=[jax.ShapeDtypeStruct(shape, dtype) for sh...  422 us
    pallas_call x4, Pallas kernels, local_kernel(): pl.pallas_call(body, out_shape=[jax.ShapeDtypeStruct(shape, dtype) for sh...  33.8 us
    unnamed x78, local copies, waits for them, and re-layouts  22.9 us
  transfers between devices with their start and end apart: 1, of which 1 were waited for; matrix products, arithmetic and copies ran while one was open for 5% of the time, Pallas kernels for 11%

profile of v2, /device:TPU:1, one launch (start us, length us, event | category | flops | bytes accessed | tf_op | source)
XLA Modules:
  0.0 590.4 jit_solution(13399332656896746422)
XLA Ops:
  7.3 2.0 fusion.25
  20.8 57.0 %shard_map.172 = (bf16[8,288,128]{2,1,0:T(8,128)(2,1)}, bf16[8,144,128]{2,1,0:T(8,128)(2,1)}, bf16[8,216,128]{2,1,0:T(8,128)(2,1)}, bf16[4,512,512]{2,1,0:T(8,128)(2,1)}, f32[8,8,128]{2,1,0:T(8,128)}) custom-call(bf16[8,288,128]{2,1,0:T(8,128)(2,1)} %pad_maximum_fusion.1.refs_0_, bf16[8,144,128]{2,1,0:T(8,128)(2,1)} %pad_maximum_fusion.3.refs_1_, ...), custom_call_target="tpu_custom_call" | custom-call | tf_op jit(solution)/shard_map/pallas_call | solution.py:83
  79.5 2.2 copy.69
  81.7 2.0 copy.70
  89.9 2.0 copy.99
  92.0 2.0 reshape.174
  93.9 1.8 pad.17.cot_ref
  95.7 1.8 pad.15.fields_ref
  98.6 6.9 %shard_map.173 = (bf16[432,512]{1,0:T(8,128)(2,1)S(1)}, bf16[432,512]{1,0:T(8,128)(2,1)S(1)}) custom-call(s32[1]{0:T(128)} %bitcast.13.cut_ref, bf16[432,512]{1,0:T(8,128)(2,1)S(1)} %copy-done.6, f32[1,512]{1,0:T(1,128)S(1)} %reshape_squeeze.3.gain_ref, bf16[4,512,512]{2,1,0:T(8,128)(2,1)S(1)} %copy-done.3), custom_call_target="tpu_custom_call" | custom-call | tf_op jit(solution)/shard_map/pallas_call | solution.py:98
  107.1 11.5 %all-gather.3.cloned.1.call-done = bf16[8,256,1024]{2,1,0:T(8,128)(2,1)} async-done(((bf16[8,32,1024]{2,1,0:T(8,128)(2,1)}), bf16[8,256,1024]{2,1,0:T(8,128)(2,1)}) %all-gather.3.cloned.1.call-update) | async-done | bytes 4194320 | tf_op jit(solution)/shard_map/all_gather | solution.py:382
  118.6 143.4 %shard_map.174 = (bf16[3,4,72,512]{3,2,1,0:T(8,128)(2,1)}, bf16[8,8,64,1024]{3,2,1,0:T(8,128)(2,1)}) custom-call(bf16[2,3,72,512]{3,2,1,0:T(8,128)(2,1)} %bitcast.90, bf16[8,8,32,1024]{3,2,1,0:T(8,128)(2,1)} %bitcast.100), custom_call_target="tpu_custom_call" | custom-call | tf_op jit(solution)/shard_map/pallas_call | solution.py:83
  264.9 2.6 reshape.147
  267.6 1.9 constant_dynamic-slice_fusion.1
  269.5 2.1 reshape.148
  271.6 1.9 copy.100
  273.5 2.0 reshape.175
  278.6 5.0 shard_map.175
  285.9 53.2 %shard_map.176 = bf16[8,112,2048]{2,1,0:T(8,128)(2,1)} custom-call(bf16[112,2048]{1,0:T(8,128)(2,1)} %copy-done.15), custom_call_target="tpu_custom_call" | custom-call | tf_op jit(solution)/shard_map/pallas_call | solution.py:83
  339.1 3.0 fusion.13
  342.2 2.4 fusion.18
  344.6 2.1 fusion.6
  347.9 2.3 fusion.15
  351.3 2.1 pad_maximum_fusion.refs_0_
  353.5 62.6 %shard_map.177.parts_ref = bf16[8,112,2048]{2,1,0:T(8,128)(2,1)} custom-call(bf16[8,112,2048]{2,1,0:T(8,128)(2,1)} %pad_maximum_fusion.refs_0_), custom_call_target="tpu_custom_call" | custom-call | tf_op jit(solution)/shard_map/pallas_call | solution.py:83
  416.1 2.0 copy-done.2
  420.1 7.2 %shard_map.178 = (bf16[8,224,128]{2,1,0:T(8,128)(2,1)S(1)}, bf16[4,112,512]{2,1,0:T(8,128)(2,1)S(1)}) custom-call(bf16[8,112,2048]{2,1,0:T(8,128)(2,1)S(1)} %copy-done.2, bf16[112,1024]{1,0:T(8,128)(2,1)S(1)} %get-tuple-element.39.merged_ref, f32[112,1024]{1,0:T(8,128)S(1)} %copy-done.14, bf16[4,112,512]{2,1,0:T(8,128)(2,1)S(1)} %copy-done.12, ...), custom_call_target="tpu_custom_call" | custom-call | tf_op jit(solution)/shard_map/pallas_call | solution.py:98
  429.9 30.6 %shard_map.179 = (bf16[3,4,72,512]{3,2,1,0:T(8,128)(2,1)}, bf16[8,224,128]{2,1,0:T(8,128)(2,1)}) custom-call(bf16[2,3,72,512]{3,2,1,0:T(8,128)(2,1)} %reshape.157.refs_0_, bf16[8,224,128]{2,1,0:T(8,128)(2,1)} %copy-done.10), custom_call_target="tpu_custom_call" | custom-call | tf_op jit(solution)/shard_map/pallas_call | solution.py:83
  466.4 2.3 copy.96
  478.2 14.7 %shard_map.180 = (bf16[8,216,128]{2,1,0:T(8,128)(2,1)S(1)}, bf16[4,512,512]{2,1,0:T(8,128)(2,1)S(1)}) custom-call(s32[1]{0:T(128)} %bitcast.13.cut_ref, bf16[432,512]{1,0:T(8,128)(2,1)S(1)} %copy-done.7, f32[1,512]{1,0:T(1,128)S(1)} %reshape_squeeze.3.gain_ref, bf16[4,512,512]{2,1,0:T(8,128)(2,1)S(1)} %copy-done.3, bf16[432,512]{1,0:T(8,128)(2,1)S(1)} %copy-done.19, ...), custom_call_target="tpu_custom_call" | custom-call | tf_op jit(solution)/shard_map/pallas_call | solution.py:98
  495.0 65.9 %shard_map.181 = (bf16[8,216,128]{2,1,0:T(8,128)(2,1)}, bf16[8,216,128]{2,1,0:T(8,128)(2,1)}, bf16[8,4,64,512]{3,2,1,0:T(8,128)(2,1)}, bf16[16,64,512]{2,1,0:T(8,128)(2,1)}, bf16[16,64,512]{2,1,0:T(8,128)(2,1)}) custom-call(bf16[8,216,128]{2,1,0:T(8,128)(2,1)} %copy-done.16, bf16[4,512,512]{2,1,0:T(8,128)(2,1)} %copy-done.8, bf16[16,64,512]{2,1,0:T(8,128)(2,1)} %bitcast.128, ...), custom_call_target="tpu_custom_call" | custom-call | tf_op jit(solution)/shard_map/pallas_call | solution.py:83
  563.8 9.1 %shard_map.182 = bf16[16,32,256]{2,1,0:T(8,128)(2,1)} custom-call(bf16[16,32,256]{2,1,0:T(8,128)(2,1)} %bitcast.126), custom_call_target="tpu_custom_call" | custom-call | tf_op jit(solution)/shard_map/pallas_call | solution.py:83
  580.8 2.5 convert_reduce_fusion
  (149 shorter events, 63.8 us)
Async XLA Ops:
  7.2 337.4 %copy-start = (bf16[1024,512]{1,0:T(8,128)(2,1)S(1)}, bf16[1024,512]{1,0:T(8,128)(2,1)}, u32[]{:S(2)}) copy-start(bf16[1024,512]{1,0:T(8,128)(2,1)} %param.21) | copy-start | bytes 3145732
  7.2 2.1 copy-start.25
  7.2 111.4 %all-gather.3.cloned.1.call-start = ((), (), s32[]{:S(2)}) async-start(), calls=%async_computation | async-start | bytes 4718592 | tf_op jit(solution)/shard_map/all_gather | solution.py:382
  10.5 2.3 copy-start.26
  15.6 1.3 copy-start.30
  15.6 1.3 copy-start.31
  15.7 2.0 copy-start.23
  81.7 2.7 copy-start.27
  85.1 1.4 copy-start.29
  89.9 7.7 %copy-start.3 = (bf16[4,512,512]{2,1,0:T(8,128)(2,1)S(1)}, bf16[4,512,512]{2,1,0:T(8,128)(2,1)}, u32[]{:S(2)}) copy-start(bf16[4,512,512]{2,1,0:T(8,128)(2,1)} %get-tuple-element.33.weights_ref) | copy-start | bytes 6291460
  97.6 1.0 copy-start.6
  105.5 0.8 copy-start.17
  106.3 0.8 copy-start.18
  269.5 7.0 %copy-start.20 = (f32[1024]{0:T(1024)S(1)}, f32[1024]{0:T(1024)}, u32[]{:S(2)}) copy-start(f32[1024]{0:T(1024)} %param.19) | copy-start | bytes 12292
  276.5 1.0 copy-start.4
  277.5 1.0 copy-start.9
  284.3 0.8 copy-start.13
  285.1 0.8 copy-start.15
  339.1 3.1 copy-start.21
  347.9 2.3 copy-start.34
  353.5 62.6 %copy-start.5 = (bf16[4,112,512]{2,1,0:T(8,128)(2,1)S(1)}, bf16[4,112,512]{2,1,0:T(8,128)(2,1)}, u32[]{:S(2)}) copy-start(bf16[4,112,512]{2,1,0:T(8,128)(2,1)} %pad.17.cot_ref) | copy-start | bytes 1376260
  416.1 2.0 copy-start.2
  418.1 1.0 copy-start.12
  419.1 1.0 copy-start.14
  427.3 0.8 copy-start.10
  474.0 3.2 copy-start.7
  477.2 1.0 copy-start.19
  492.9 1.3 copy-start.8
  560.9 1.7 copy-start.24
  563.0 12.4 %copy-start.28 = (bf16[8,216,128]{2,1,0:T(8,128)(2,1)S(1)}, bf16[8,216,128]{2,1,0:T(8,128)(2,1)}, u32[]{:S(2)}) copy-start(bf16[8,216,128]{2,1,0:T(8,128)(2,1)} %get-tuple-element.50) | copy-start | bytes 1327108
  576.5 1.1 copy-start.22
  579.1 4.2 copy-start.1
  (4 other events, 2.9 us)
Sparse Core Ops, SparseCore 0:
  10.4 108.1 all-gather.2
